TPU v7x, 32 devices: a whole 2x2x4 slice. The times are simulated.
32 devices in a mesh: ctx: 8 (over y, x, core), head: 4 (over z).
Axes of the slice: x: 2, y: 2, z: 4, core: 2. Of those that a mesh axis runs over, the one named last changes fastest.
Arguments:
- query_raw: bfloat16 [4096, 2048], P('ctx', 'head'), may hold values from -120 to 120
- key_raw: bfloat16 [4096, 2048], P('ctx', 'head'), may hold values from -120 to 120
- value_raw: bfloat16 [4096, 4096], P('ctx', 'head'), may hold values from -120 to 120
- conv_query: bfloat16 [4, 2048], P(None, 'head'), may hold values from -3 to 3
- conv_key: bfloat16 [4, 2048], P(None, 'head'), may hold values from -3 to 3
- conv_value: bfloat16 [4, 4096], P(None, 'head'), may hold values from -3 to 3
- decay_log: float32 [32, 4096], P('head', 'ctx'), may hold values from -0.6 to 0, as said below
- write_beta: float32 [32, 4096], P('head', 'ctx'), may hold values from 0 to 1
- gate_input: bfloat16 [4096, 4096], P('ctx', 'head'), may hold values from -6 to 6
- norm_gain: float32 [128], replicated, may hold values from 0.5 to 1.5
- out_weight: bfloat16 [4096, 2048], P('head'), may hold values from -0.125 to 0.125
Outputs:
- mixed: bfloat16 [4096, 2048], P('ctx', 'head')
Inputs may be any that keep to these rules, and one draw needn't show every extreme that they name: `decay_log`: natural logarithm of a decay factor.
All inputs are finite; a program needn't handle non-finite values.
Results may differ from a plain program's by a relative error of at most 0.014.
Values may be sent and summed in bfloat16 or wider, within the bound.
A program may use at most 128 MiB of HBM per device.

v0:
```python
import jax
import jax.numpy as jnp
from jax import lax
from jax.sharding import PartitionSpec as P

DK = 128
DV = 128
CONV = 4
BLOCK = 64


highest = lax.Precision.HIGHEST


def shifted(value, axis, by):
    length = lax.axis_size(axis)
    pairs = [(i, i + by) for i in range(length) if 0 <= i + by < length]
    return lax.ppermute(value, axis, pairs)


def prefix(value, axis, combine, identity):
    length, place = (lax.axis_size(axis), lax.axis_index(axis))
    everything = jax.tree.map(
        lambda part, kind: lax.all_gather(part.astype(kind), axis),
        value,
        (jnp.bfloat16, jnp.bfloat16),
    )
    start = jax.tree.map(
        lambda part, zero: jnp.broadcast_to(jnp.asarray(zero, part.dtype), part.shape),
        value,
        identity,
    )

    def lap(k, before):
        reached = k < place
        new = combine(
            before, jax.tree.map(lambda part, own: part[k].astype(own.dtype), everything, value)
        )
        return jax.tree.map(lambda a, b: jnp.where(reached, a, b), new, before)

    return lax.fori_loop(0, length, lap, start)


def conv_silu(raw_rows, rim_rows, conv_weight):
    widths = conv_weight.shape[0]
    length = raw_rows.shape[0]
    padded = jnp.concatenate([rim_rows.astype(jnp.float32), raw_rows.astype(jnp.float32)], 0)
    weights = conv_weight.astype(jnp.float32)
    running = jnp.zeros((length, raw_rows.shape[1]), jnp.float32)
    for offset in range(widths):
        running = running + weights[offset] * padded[offset : offset + length]
    return jax.nn.silu(running)


def unit_rows(values):
    return values * lax.rsqrt(jnp.sum(values * values, -1, keepdims=True) + 1e-06)


def prepare(key_block, value_block, cumulative, beta_blocks):
    length = key_block.shape[-2]
    inner_keys = jnp.einsum("...id,...jd->...ij", key_block, key_block, precision=highest)
    positions = jnp.arange(length)
    strict_lower = positions[:, None] > positions[None, :]
    causal = positions[:, None] >= positions[None, :]
    spread = jnp.exp(jnp.where(causal, cumulative[..., :, None] - cumulative[..., None, :], 0.0))
    lower_part = jnp.where(strict_lower, beta_blocks[..., :, None] * inner_keys * spread, 0.0)
    system = jnp.eye(length, dtype=jnp.float32) + lower_part
    key_mix = jax.scipy.linalg.solve_triangular(
        system, (beta_blocks * jnp.exp(cumulative))[..., None] * key_block, lower=True
    )
    value_mix = jax.scipy.linalg.solve_triangular(
        system, beta_blocks[..., None] * value_block, lower=True
    )
    return (key_mix, value_mix, spread, causal)


def block_outputs(
    carry_state, query_block, key_block, key_mix, value_mix, cumulative, spread, causal
):
    fresh_values = value_mix - jnp.einsum("hcd,hvd->hcv", key_mix, carry_state, precision=highest)
    scores = jnp.where(
        causal, jnp.einsum("hid,hjd->hij", query_block, key_block, precision=highest) * spread, 0.0
    )
    result = jnp.einsum(
        "hcd,hvd->hcv", query_block * jnp.exp(cumulative)[..., None], carry_state, precision=highest
    )
    result = result + jnp.einsum("hij,hjv->hiv", scores, fresh_values, precision=highest)
    last_cum = cumulative[:, -1]
    carried = jnp.exp(last_cum[:, None] - cumulative)[..., None] * fresh_values
    carry_state = jnp.exp(last_cum)[:, None, None] * carry_state + jnp.einsum(
        "hcv,hcd->hvd", carried, key_block, precision=highest
    )
    return (carry_state, result)


def batch_product(left_side, right_side):
    return jnp.einsum("hab,hbc->hac", left_side, right_side, precision=highest)


def body(
    query_raw,
    key_raw,
    value_raw,
    conv_query,
    conv_key,
    conv_value,
    decay_log,
    write_beta,
    gate_input,
    norm_gain,
    out_weight,
):
    local_tokens = query_raw.shape[0]
    key_heads = query_raw.shape[1] // DK
    value_heads = value_raw.shape[1] // DV
    head_ratio = value_heads // key_heads
    block_count = local_tokens // BLOCK
    margin = CONV - 1
    rim_rows = shifted(
        (
            query_raw[local_tokens - margin :],
            key_raw[local_tokens - margin :],
            value_raw[local_tokens - margin :],
        ),
        "ctx",
        1,
    )
    queries = unit_rows(
        conv_silu(query_raw, rim_rows[0], conv_query).reshape(local_tokens, key_heads, DK)
    ) * DK ** (-0.5)
    key_unit = unit_rows(
        conv_silu(key_raw, rim_rows[1], conv_key).reshape(local_tokens, key_heads, DK)
    )
    values = conv_silu(value_raw, rim_rows[2], conv_value).reshape(local_tokens, value_heads, DV)

    def blocks(array, heads, width):
        return array.reshape(block_count, BLOCK, heads, width).transpose(0, 2, 1, 3)

    query_blocks = jnp.repeat(blocks(queries, key_heads, DK), head_ratio, axis=1)
    key_blocks = jnp.repeat(blocks(key_unit, key_heads, DK), head_ratio, axis=1)
    value_blocks = blocks(values, value_heads, DV)
    cumulative = jnp.cumsum(
        decay_log.reshape(value_heads, block_count, BLOCK).transpose(1, 0, 2), axis=-1
    )
    beta_blocks = write_beta.reshape(value_heads, block_count, BLOCK).transpose(1, 0, 2)
    key_mix, value_mix, spread, causal = prepare(key_blocks, value_blocks, cumulative, beta_blocks)
    identity = jnp.broadcast_to(jnp.eye(DK, dtype=jnp.float32), (value_heads, DK, DK))
    empty_state = jnp.zeros((value_heads, DV, DK), jnp.float32)

    def compose(carry, inputs):
        transit, offset = carry
        key_block, mix_block, value_block, cumul_block = inputs
        last_cum = cumul_block[:, -1]
        tail_weight = jnp.exp(last_cum[:, None] - cumul_block)[..., None]
        step_transit = jnp.exp(last_cum)[:, None, None] * identity - jnp.einsum(
            "hcd,hce->hde", mix_block * tail_weight, key_block, precision=highest
        )
        step_offset = jnp.einsum(
            "hcv,hce->hve", value_block * tail_weight, key_block, precision=highest
        )
        return (
            (
                batch_product(transit, step_transit),
                batch_product(offset, step_transit) + step_offset,
            ),
            None,
        )

    (transit, offset), unused = lax.scan(
        compose, (identity, empty_state), (key_blocks, key_mix, value_mix, cumulative)
    )

    def combine(earlier, later):
        return (batch_product(earlier[0], later[0]), batch_product(earlier[1], later[0]) + later[1])

    start_state = prefix((transit, offset), "ctx", combine, (identity, empty_state))[1]

    def advance(carry_state, inputs):
        query_block, key_block, mix_block, value_block, cumul_block, spread_block = inputs
        return block_outputs(
            carry_state,
            query_block,
            key_block,
            mix_block,
            value_block,
            cumul_block,
            spread_block,
            causal,
        )

    final_state, outputs = lax.scan(
        advance, start_state, (query_blocks, key_blocks, key_mix, value_mix, cumulative, spread)
    )
    heads_out = outputs.transpose(0, 2, 1, 3).reshape(local_tokens, value_heads, DV)
    normed = heads_out * lax.rsqrt(jnp.mean(heads_out * heads_out, -1, keepdims=True) + 1e-06)
    gated = (
        normed
        * norm_gain
        * jax.nn.silu(gate_input.astype(jnp.float32).reshape(local_tokens, value_heads, DV))
    )
    hidden = gated.astype(jnp.bfloat16).reshape(local_tokens, value_heads * DV)
    summed = lax.psum_scatter(
        lax.dot_general(
            out_weight, hidden, (((0,), (1,)), ((), ())), preferred_element_type=jnp.float32
        ).astype(jnp.bfloat16),
        "head",
        scatter_dimension=0,
        tiled=True,
    ).astype(jnp.float32)
    return jnp.transpose(summed).astype(jnp.bfloat16)


def solution(mesh):
    return jax.shard_map(
        body,
        mesh=mesh,
        in_specs=(
            P("ctx", "head"),
            P("ctx", "head"),
            P("ctx", "head"),
            P(None, "head"),
            P(None, "head"),
            P(None, "head"),
            P("head", "ctx"),
            P("head", "ctx"),
            P("ctx", "head"),
            P(),
            P("head", None),
        ),
        out_specs=P("ctx", "head"),
        check_vma=False,
    )
```

profile of v0, /device:TPU:0, one launch (start us, length us, event | category | flops | bytes accessed | tf_op | source)
XLA Modules:
  0.0 655.4 jit_solution(12860872139963788723)
XLA Ops:
  7.3 2.3 collective-permute-start
  10.4 4.5 collective-permute-start.1
  26.1 4.8 select_bitcast_fusion
  30.9 316.0 %custom-call.6 = f32[8,8,1,64,64]{3,4,2,1,0:T(8,128)} custom-call(f32[8,8,1,64,64]{4,3,2,1,0:T(8,128)} %select_bitcast_fusion), custom_call_target="InvertDiagBlocksLowerTriangular" | custom-call | tf_op jit(solution)/shard_map/jit(_solve_triangular)/vmap(vmap())/triangular_solve | solution.py:68
  346.9 7.1 %fusion.63 = f32[8,8,64,128]{3,2,1,0:T(8,128)} fusion(f32[8,8,1,64,64]{3,4,2,1,0:T(8,128)} %custom-call.6, f32[8,8,64,128]{3,2,1,0:T(8,128)S(1)} %bitcast.192, f32[8,8,64]{2,1,0:T(8,128)S(1)} %exponential_multiply_fusion), kind=kOutput, calls=%fused_computation.89 | convolution fusion | flops 403177472 | bytes 5259264 | tf_op jit(solution)/shard_map/jit(_solve_triangular)/vmap(vmap())/triangular_solve | solution.py:68
  357.1 5.4 fusion.61
  362.5 66.0 %while.41 = (s32[]{:T(128)}, f32[8,128,128]{1,2,0:T(8,128)S(1)}, f32[8,128,128]{1,2,0:T(8,128)}, f32[8,8,64]{2,1,0:T(8,128)S(1)}, f32[8,8,64,128]{3,2,1,0:T(8,12...) while((s32[]{:T(128)}, f32[8,128,128]{1,2,0:T(8,128)S(1)}, ...), condition=%wide.region_3.5_spmd.clone, body=%wide.region_2.4_spmd.clone.sunk | while | flops 604635648 | bytes 6900511 | solution.py:169
  362.8 2.1 convolution_subtract_fusion.5
  367.1 2.8 convolution_add_fusion.6
  370.2 2.1 convolution_subtract_fusion.5
  373.3 2.1 convolution_bitcast_fusion.6
  375.4 2.8 convolution_add_fusion.6
  378.6 2.1 convolution_subtract_fusion.5
  381.7 2.1 convolution_bitcast_fusion.6
  383.8 2.8 convolution_add_fusion.6
  386.9 2.1 convolution_subtract_fusion.5
  390.1 2.1 convolution_bitcast_fusion.6
  392.2 2.8 convolution_add_fusion.6
  395.3 2.1 convolution_subtract_fusion.5
  398.5 2.1 convolution_bitcast_fusion.6
  400.6 2.8 convolution_add_fusion.6
  403.7 2.1 convolution_subtract_fusion.5
  406.9 2.1 convolution_bitcast_fusion.6
  409.0 2.8 convolution_add_fusion.6
  412.1 2.1 convolution_subtract_fusion.5
  415.2 2.1 convolution_bitcast_fusion.6
  417.3 2.8 convolution_add_fusion.6
  420.5 2.1 convolution_subtract_fusion.5
  423.6 2.1 convolution_bitcast_fusion.6
  425.7 2.8 convolution_add_fusion.6
  437.3 2.0 fusion.93
  439.2 2.7 reshape.156
  447.2 10.6 %all-gather.5.cloned.1.call-done = bf16[64,128,128]{2,1,0:T(8,128)(2,1)} async-done(((bf16[8,128,128]{2,1,0:T(8,128)(2,1)}), bf16[64,128,128]{2,1,0:T(8,128)(2,1)}) %all-gather.5.cloned.1.call-update) | async-done | bytes 2097168 | tf_op jit(solution)/shard_map/all_gather | solution.py:24
  457.8 29.8 %all-gather.7.cloned.1.call-done = bf16[64,128,128]{2,1,0:T(8,128)(2,1)} async-done(((bf16[8,128,128]{2,1,0:T(8,128)(2,1)}), bf16[64,128,128]{2,1,0:T(8,128)(2,1)}) %all-gather.7.cloned.1.call-update) | async-done | bytes 2097168 | tf_op jit(solution)/shard_map/all_gather | solution.py:24
  487.6 35.9 %while.42 = (s32[]{:T(128)}, f32[8,128,128]{1,2,0:T(8,128)}, s32[]{:T(128)}, bf16[8,8,128,128]{3,2,1,0:T(8,128)(2,1)}, bf16[8,8,128,128]{3,2,1,0:T(8,128)(2,1)}, /*index=5*/s32[]{:T(128)}, s32[]{:T(128)}) while((s32[]{:T(128)}, f32[8,128,128]{1,2,0:T(8,128)}, s32[]{:T(128)}, bf16[8,8,128,128]{3,2,1,0:T(8,128)(2,1)}, ...), condition=%wide.region_5.7_spmd.clone, body=%wide.region_4.6_spmd.clone.sunk | while | flops 201981952 | bytes 4196459 | solution.py:41
  489.8 2.3 fusion.151
  494.3 2.3 fusion.151
  498.8 2.3 fusion.151
  503.3 2.3 fusion.151
  507.8 2.3 fusion.151
  512.3 2.3 fusion.151
  516.8 2.3 fusion.151
  521.3 2.3 fusion.151
  524.8 2.9 broadcast_in_dim.67
  527.7 67.8 %while.40 = (s32[]{:T(128)}, f32[8,128,128]{2,1,0:T(8,128)S(1)}, f32[8,8,64,128]{3,2,1,0:T(8,128)}, f32[8,8,64]{2,1,0:T(8,128)S(1)}, f32[8,8,64,128]{3,2,1,0:T(8...) while((s32[]{:T(128)}, f32[8,128,128]{2,1,0:T(8,128)S(1)}, ...), condition=%wide.region_8.10_spmd.clone, body=%wide.region_7.9_spmd.clone.sunk | while | flops 403247616 | bytes 5799197 | solution.py:191
  527.7 2.1 fusion.140
  529.7 2.2 convolution_subtract_fusion.4
  536.1 2.1 fusion.140
  538.2 2.2 convolution_subtract_fusion.4
  544.6 2.1 fusion.140
  546.7 2.2 convolution_subtract_fusion.4
  553.1 2.1 fusion.140
  555.2 2.2 convolution_subtract_fusion.4
  561.6 2.1 fusion.140
  563.6 2.2 convolution_subtract_fusion.4
  570.0 2.1 fusion.140
  572.1 2.2 convolution_subtract_fusion.4
  578.5 2.1 fusion.140
  580.6 2.2 convolution_subtract_fusion.4
  587.0 2.1 fusion.140
  589.1 2.2 convolution_subtract_fusion.4
  595.5 2.4 multiply_reduce_fusion
  600.7 4.1 fusion.47
  604.8 44.0 %reduce-scatter.2.cloned.1.call-done = bf16[512,512]{0,1:T(8,128)(2,1)} async-done(((bf16[2048,512]{0,1:T(8,128)(2,1)}), bf16[512,512]{0,1:T(8,128)(2,1)}) %reduce-scatter.2.cloned.1.call-update) | async-done | bytes 524304 | tf_op jit(solution)/shard_map/reduce_scatter | solution.py:202
  (217 shorter events, 96.6 us)
Async XLA Ops:
  6.5 429.5 %copy-start = (f32[128]{0:T(128)S(1)}, f32[128]{0:T(128)}, u32[]{:S(2)}) copy-start(f32[128]{0:T(128)} %param.28) | copy-start | bytes 1540
  6.5 14.7 %copy-start.6 = (bf16[512,1024]{1,0:T(8,128)(2,1)S(1)}, bf16[512,1024]{1,0:T(8,128)(2,1)}, u32[]{:S(2)}) copy-start(bf16[512,1024]{1,0:T(8,128)(2,1)} %param.21) | copy-start | bytes 3145732
  6.5 451.3 %all-gather.5.cloned.1.call-start = ((), (), s32[]{:S(2)}) async-start(), calls=%async_computation.2 | async-start | bytes 2359296 | tf_op jit(solution)/shard_map/all_gather | solution.py:24
  7.3 15.6 %collective-permute-start = (bf16[3,512]{1,0:T(4,128)(2,1)S(1)}, bf16[3,512]{1,0:T(4,128)(2,1)S(1)}, u32[]{:S(2)}, u32[]{:S(2)}) collective-permute-start(bf16[3,512]{1,0:T(4,128)(2,1)S(1)} %slice.83), channel_id=1, source_target_pairs={{0,4},{4,8},{8,12},{12,16},{16,20},{20,24},{24,28},{1,5},{5,9},{9,... | collective-permute-start | bytes 9224 | tf_op jit(solution)/shard_map/ppermute | solution.py:18
  10.4 343.6 %collective-permute-start.1 = (bf16[3,1024]{1,0:T(4,128)(2,1)S(1)}, bf16[3,1024]{1,0:T(4,128)(2,1)S(1)}, u32[]{:S(2)}, u32[]{:S(2)}) collective-permute-start(bf16[3,1024]{1,0:T(4,128)(2,1)S(1)} %slice.91), channel_id=1, source_target_pairs={{0,4},{4,8},{8,12},{12,16},{16,20},{20,24},{24,28},{1,5},{5,9},{9,... | collective-permute-start | bytes 18440 | tf_op jit(solution)/shard_map/ppermute | solution.py:18
  346.9 7.1 %copy-start.3 = (f32[512,1024]{1,0:T(8,128)S(1)}, f32[512,1024]{1,0:T(8,128)}, u32[]{:S(2)}) copy-start(f32[512,1024]{1,0:T(8,128)} %convert_element_type.83) | copy-start | bytes 6291460
  355.5 1.6 copy-start.1
  428.6 5.5 copy-start.7
  429.4 58.2 %all-gather.7.cloned.1.call-start = ((), (), s32[]{:S(2)}) async-start(), calls=%async_computation.3 | async-start | bytes 2359296 | tf_op jit(solution)/shard_map/all_gather | solution.py:24
  431.4 217.5 %reduce-scatter.2.cloned.1.call-start = ((), (), s32[]{:S(2)}) async-start(), calls=%async_computation.1 | async-start | bytes 2621440 | tf_op jit(solution)/shard_map/reduce_scatter | solution.py:202
  432.2 5.1 collective-permute-start.2
  439.2 2.7 copy-start.4
  443.2 2.0 copy-start.5
  595.5 2.5 copy-start.2
  598.0 2.2 copy-start.8
  599.2 1.5 copy-start.9
Sparse Core Ops, SparseCore 0:
  429.6 28.2 all-gather.4
  459.7 27.8 all-gather.6
  605.0 43.8 reduce-scatter.1
where the time goes:
time: 659 us; the launch traced here: 655 us
  other arithmetic  335 us (51%)
  matrix products  168 us (25%)
  waiting for transfers between devices  84.5 us (13%)
  local copies, waits for them, and re-layouts  44.2 us (7%)
  between operations  13.5 us (2%)
  starting transfers between devices  8.83 us (1%)
    another operation x2, other arithmetic, prepare(): jax.scipy.linalg.solve_triangular(system, (beta_blocks * jnp.exp(cumulati...  316 us
    reduce_scatter x1, waiting for transfers between devices, body(): lax.psum_scatter(lax.dot_general(out_weight, hidden, (((0,), (1,)), ((),...  44 us
    dot_general x24, matrix products, batch_product(): return jnp.einsum('hab,hbc->hac', left_side, right_side, precision=highest)  42.2 us
    all_gather x2, waiting for transfers between devices, prefix(): lax.all_gather(part.astype(kind), axis)  40.5 us
    dot_general x8, matrix products, compose(): jnp.einsum('hcv,hce->hve', value_block * tail_weight, key_block, precisio...  22.8 us
    dot_general x8, matrix products, block_outputs(): jnp.einsum('hcd,hvd->hcv', key_mix, carry_state, precision=highest)  17.3 us
    dot_general x8, matrix products, block_outputs(): jnp.einsum('hcd,hvd->hcv', query_block * jnp.exp(cumulative)[..., None],...  16.6 us
    dot_general x8, matrix products, compose(): jnp.einsum('hcd,hce->hde', mix_block * tail_weight, key_block, precision=...  16.5 us
  transfers between devices with their start and end apart: 6, of which 3 were waited for; matrix products, arithmetic and copies ran while one was open for 54% of the time, Pallas kernels for 0%

commit v1 on v0

v1 whole, which is shorter than its diff:
```python
import functools

import jax
import jax.numpy as jnp
from jax import lax
from jax.experimental import pallas as pl
from jax.experimental.pallas import tpu as pltpu
from jax.sharding import PartitionSpec as P

DK = 128
DV = 128
CONV = 4
BLOCK = 64
CHUNK = 2 * BLOCK
RIM = 16
F32 = jnp.float32
BF16 = jnp.bfloat16


def mm(a, b):
    return jnp.dot(a.astype(BF16), b.astype(BF16), preferred_element_type=F32)


def mm_nt(a, b):
    return lax.dot_general(
        a.astype(BF16), b.astype(BF16), (((1,), (1,)), ((), ())), preferred_element_type=F32
    )


def silu(x):
    return x / (1.0 + jnp.exp(-x))


def iota(shape, dim):
    return lax.broadcasted_iota(jnp.int32, shape, dim)


def conv_part(tail, rows, taps):
    whole = jnp.concatenate([tail, rows], 0)
    first = 8 - (CONV - 1)
    total = taps[0:1] * whole[first : first + CHUNK]
    for j in range(1, CONV):
        total = total + taps[j : j + 1] * whole[first + j : first + j + CHUNK]
    return silu(total)


def unit(x, scale):
    return x * (lax.rsqrt(jnp.sum(x * x, -1, keepdims=True) + 1e-06) * scale)


def local_kernel(
    q_ref, k_ref, v_ref, rim_ref, cq_ref, ck_ref, cv_ref, dec_ref, beta_ref,
    out_ref, qeff_ref, trans_ref,
    tail_ref, bd_ref, st_ref,
):
    tokens = q_ref.shape[0]
    key_heads = q_ref.shape[1] // DK
    heads = v_ref.shape[1] // DV
    ratio = heads // key_heads
    width = ratio * CHUNK
    qc, kc = q_ref.shape[1], k_ref.shape[1]

    tail_ref[...] = rim_ref[...].astype(F32)[RIM - 8 :]
    bd_ref[...] = (
        iota((width, width), 0) // BLOCK == iota((width, width), 1) // BLOCK
    ).astype(F32).astype(BF16)
    for h in range(heads):
        st_ref[h] = jnp.concatenate(
            [jnp.zeros((DK, DV), F32), (iota((DK, DK), 0) == iota((DK, DK), 1)).astype(F32)], 1
        )

    def diag(value):
        return jnp.concatenate([value] * (width // BLOCK), 0) * bd_ref[...]

    def step(c, unused):
        at = pl.ds(pl.multiple_of(c * CHUNK, CHUNK), CHUNK)
        row = iota((BLOCK, width), 0)
        lane = iota((BLOCK, width), 1)
        col = lane % BLOCK
        half = iota((BLOCK, CHUNK), 1) < BLOCK
        row1, col1 = iota((BLOCK, CHUNK), 0), iota((BLOCK, CHUNK), 1) % BLOCK
        eye = (row == col).astype(F32)

        dec = dec_ref[:, at]
        beta = beta_ref[:, at]
        tri = (
            (iota((CHUNK, CHUNK), 0) <= iota((CHUNK, CHUNK), 1))
            & (iota((CHUNK, CHUNK), 0) // BLOCK == iota((CHUNK, CHUNK), 1) // BLOCK)
        ).astype(F32)
        cum = jnp.dot(dec, tri, precision=lax.Precision.HIGHEST, preferred_element_type=F32)
        last = jnp.where(
            iota((heads, CHUNK), 1) < BLOCK, cum[:, BLOCK - 1 : BLOCK], cum[:, CHUNK - 1 : CHUNK]
        )
        grow = jnp.exp(cum)
        rows = jnp.concatenate(
            [cum, beta, beta * grow, grow, jnp.exp(last - cum)], 0
        )
        cols = jnp.transpose(
            jnp.concatenate([rows, jnp.zeros((CHUNK - rows.shape[0], CHUNK), F32)], 0)
        )

        def column(kind, h):
            return cols[:, kind * heads + h : kind * heads + h + 1]

        def compact(x):
            return jnp.where(half, x[:BLOCK], x[BLOCK:])

        def conv(ref, taps_ref, offset, part):
            s = pl.ds(part * DK, DK)
            t = pl.ds(offset + part * DK, DK)
            new = ref[at, s].astype(F32)
            result = conv_part(tail_ref[:, t], new, taps_ref[:, s].astype(F32))
            tail_ref[:, t] = new[CHUNK - 8 :]
            return result

        queries, keys, lowers, scores, values = [], [], [], [], []
        for kh in range(key_heads):
            q = unit(conv(q_ref, cq_ref, 0, kh), DK ** (-0.5))
            k = unit(conv(k_ref, ck_ref, qc, kh), 1.0)
            kk = compact(mm_nt(k, k))
            qk = compact(mm_nt(q, k))
            low = []
            for g in range(ratio):
                h = kh * ratio + g
                values.append(conv(v_ref, cv_ref, qc + kc, h))
                cc = compact(jnp.broadcast_to(column(0, h), (CHUNK, CHUNK)))
                bc = compact(jnp.broadcast_to(column(1, h), (CHUNK, CHUNK)))
                spread = jnp.exp(jnp.where(row1 >= col1, cc - cum[h : h + 1], 0.0))
                low.append(jnp.where(row1 > col1, bc * kk * spread, 0.0))
                scores.append(jnp.where(row1 >= col1, qk * spread, 0.0).astype(BF16))
            lowers.append(jnp.concatenate(low, 1))
            queries.append(q)
            keys.append(k)

        inverse = [eye - jnp.where(row // 2 == col // 2, low, 0.0) for low in lowers]
        size = 2
        while size < BLOCK:
            off = (row // (2 * size) == col // (2 * size)) & (row // size > col // size)
            left = [
                mm(x, diag(jnp.where(off, low, 0.0).astype(BF16)))
                for x, low in zip(inverse, lowers)
            ]
            inverse = [x - mm(p, diag(x.astype(BF16))) for x, p in zip(inverse, left)]
            size *= 2

        mixes = []
        for kh in range(key_heads):
            rhs = []
            for g in range(ratio):
                h = kh * ratio + g
                rhs.append(
                    jnp.concatenate([column(2, h) * keys[kh], column(1, h) * values[h]], 1)
                )
            mixes.append(mm(diag(inverse[kh].astype(BF16)), jnp.concatenate(rhs, 0)))

        firsts, seconds = [], []
        for h in range(heads):
            kh, g = h // ratio, h % ratio
            firsts.append((column(3, h) * queries[kh]).astype(BF16))
            turned = jnp.transpose(column(4, h) * keys[kh]).astype(BF16)
            seconds.append(jnp.concatenate([scores[h], turned], 0))

        for s in range(CHUNK // BLOCK):
            one = []
            for h in range(heads):
                kh, g = h // ratio, h % ratio
                mix = mixes[kh][g * CHUNK + s * BLOCK : g * CHUNK + (s + 1) * BLOCK]
                lhs = jnp.concatenate(
                    [mix[:, :DK].astype(BF16), firsts[h][s * BLOCK : (s + 1) * BLOCK]], 0
                )
                one.append((mm(lhs, st_ref[h]), mix[:, DK:]))
            for h in range(heads):
                r1, u = one[h]
                fresh = jnp.concatenate([u - r1[:BLOCK, :DV], -r1[:BLOCK, DV:]], 1).astype(BF16)
                zero = jnp.zeros_like(fresh)
                r2 = mm(seconds[h], jnp.concatenate([fresh, zero] if s == 0 else [zero, fresh], 0))
                result = r1[BLOCK:] + r2[:BLOCK]
                where = pl.ds(pl.multiple_of(c * CHUNK + s * BLOCK, BLOCK), BLOCK)
                out_ref[where, h * DV : (h + 1) * DV] = result[:, :DV]
                qeff_ref[where, h * DK : (h + 1) * DK] = result[:, DV:].astype(BF16)
                decay = jnp.exp(cum[h : h + 1, (s + 1) * BLOCK - 1 : (s + 1) * BLOCK])
                st_ref[h] = decay * st_ref[h] + r2[BLOCK:]
        return unused

    lax.fori_loop(0, tokens // CHUNK, step, 0)
    trans_ref[...] = st_ref[...].astype(BF16)


def finish_kernel(
    out_ref, qeff_ref, every_ref, gate_ref, gain_ref, weight_ref, part_ref, start_ref, hid_ref
):
    heads = every_ref.shape[1]
    tokens = out_ref.shape[0]
    place = lax.axis_index("ctx")
    start_ref[...] = jnp.zeros_like(start_ref)

    def lap(i, unused):
        for h in range(heads):
            state = start_ref[h]
            high = state.astype(BF16)
            low = (state - high.astype(F32)).astype(BF16)
            moved = mm(every_ref[i, h, :, DV:], jnp.concatenate([high, low], 1))
            start_ref[h] = moved[:, :DV] + moved[:, DV:] + every_ref[i, h, :, :DV].astype(F32)
        return unused

    lax.fori_loop(0, place, lap, 0)
    gain = gain_ref[...]
    rows = 128

    def chunk(c, unused):
        at = pl.ds(pl.multiple_of(c * rows, rows), rows)
        for h in range(heads):
            cs = slice(h * DV, (h + 1) * DV)
            o = out_ref[at, cs] + mm(qeff_ref[at, cs], start_ref[h])
            n = o * lax.rsqrt(jnp.mean(o * o, -1, keepdims=True) + 1e-06)
            hid_ref[at, cs] = (n * gain * silu(gate_ref[at, cs].astype(F32))).astype(BF16)
        hidden = hid_ref[at, :]
        width = part_ref.shape[2]
        for d in range(part_ref.shape[0]):
            part_ref[d, at, :] = mm(hidden, weight_ref[:, d * width : (d + 1) * width]).astype(BF16)
        return unused

    lax.fori_loop(0, tokens // rows, chunk, 0)


def body(
    query_raw, key_raw, value_raw, conv_query, conv_key, conv_value,
    decay_log, write_beta, gate_input, norm_gain, out_weight,
):
    tokens = query_raw.shape[0]
    heads = value_raw.shape[1] // DV
    ratio = value_raw.shape[1] // key_raw.shape[1]
    channels = query_raw.shape[1] + key_raw.shape[1] + value_raw.shape[1]
    n_ctx, n_head = lax.axis_size("ctx"), lax.axis_size("head")
    rim = lax.ppermute(
        jnp.concatenate([x[tokens - RIM :] for x in (query_raw, key_raw, value_raw)], 1),
        "ctx",
        [(i, i + 1) for i in range(n_ctx - 1)],
    )
    vmem = pl.BlockSpec(memory_space=pltpu.VMEM)
    out, qeff, trans = pl.pallas_call(
        local_kernel,
        out_shape=(
            jax.ShapeDtypeStruct((tokens, heads * DV), F32),
            jax.ShapeDtypeStruct((tokens, heads * DK), BF16),
            jax.ShapeDtypeStruct((heads, DK, DV + DK), BF16),
        ),
        in_specs=[vmem] * 9,
        out_specs=[vmem] * 3,
        scratch_shapes=[
            pltpu.VMEM((8, channels), F32),
            pltpu.VMEM((ratio * CHUNK, ratio * CHUNK), BF16),
            pltpu.VMEM((heads, DK, DV + DK), F32),
        ],
        compiler_params=pltpu.CompilerParams(vmem_limit_bytes=48 * 2**20),
        name="local",
    )(
        query_raw, key_raw, value_raw, rim, conv_query, conv_key, conv_value,
        decay_log, write_beta,
    )
    every = lax.all_gather(trans, "ctx")
    part = pl.pallas_call(
        finish_kernel,
        out_shape=jax.ShapeDtypeStruct((n_head, tokens, out_weight.shape[1] // n_head), BF16),
        in_specs=[vmem] * 6,
        out_specs=vmem,
        scratch_shapes=[
            pltpu.VMEM((heads, DK, DV), F32),
            pltpu.VMEM((tokens, heads * DV), BF16),
        ],
        compiler_params=pltpu.CompilerParams(vmem_limit_bytes=48 * 2**20),
        name="finish",
    )(out, qeff, every, gate_input, norm_gain.reshape(1, DV), out_weight)
    return lax.psum_scatter(part, "head", scatter_dimension=0)


def solution(mesh):
    return jax.shard_map(
        body,
        mesh=mesh,
        in_specs=(
            P("ctx", "head"), P("ctx", "head"), P("ctx", "head"),
            P(None, "head"), P(None, "head"), P(None, "head"),
            P("head", "ctx"), P("head", "ctx"), P("ctx", "head"),
            P(), P("head", None),
        ),
        out_specs=P("ctx", "head"),
        check_vma=False,
    )
```

time: 659 us -> 143 us (0.22)
  other arithmetic: 335 us -> 0.01 us
  matrix products: 168 us -> 0 us
  local copies, waits for them, and re-layouts: 44.2 us -> 12.2 us
  Pallas kernels: 0 us -> 25.1 us
    another operation x3 -> x0, other arithmetic: 318 us -> none  [the longest x2 316 us: prepare(): jax.scipy.linalg.solve_triangular(system, (beta_blocks * jnp.exp(cumulati...]
    dot_general x82 -> x0, matrix products: 156 us -> none  [the longest x24 42.2 us: batch_product(): return jnp.einsum('hab,hbc->hac', left_side, right_side, precision=highest)]
    pallas_call x0 -> x2, Pallas kernels: none -> 25.1 us  [the longest x1 15.4 us: body(): pl.pallas_call(local_kernel, out_shape=(jax.ShapeDtypeStruct((tokens, hea...]
    another operation x2 -> x0, matrix products: 12.5 us -> none  [the longest x1 7.1 us: prepare(): jax.scipy.linalg.solve_triangular(system, (beta_blocks * jnp.exp(cumulati...]
    while x18 -> x0, local copies, waits for them, and re-layouts: 11.4 us -> none
    dynamic_slice x16 -> x0, local copies, waits for them, and re-layouts: 9.2 us -> none  [lap(): part[k].astype(own.dtype)]
    all_gather x2 -> x1, waiting for transfers between devices: 40.5 us -> 41.9 us  [body(): every = lax.all_gather(trans, 'ctx')]
  transfers between devices with their start and end apart: 6 -> 3, of which waited for: 3 -> 3; matrix products, arithmetic and copies ran while one was open for 54% -> 0% of each run, Pallas kernels for 0% -> 0%
where the time goes in v1:
time: 143 us; the launch traced here: 142 us
  waiting for transfers between devices  88.7 us (62%)
  Pallas kernels  25.1 us (18%)
  between operations  13.4 us (9%)
  local copies, waits for them, and re-layouts  12.2 us (9%)
  starting transfers between devices  2.4 us (2%)
    reduce_scatter x1, waiting for transfers between devices, body(): return lax.psum_scatter(part, 'head', scatter_dimension=0)  46 us
    all_gather x1, waiting for transfers between devices, body(): every = lax.all_gather(trans, 'ctx')  41.9 us
    pallas_call x1, Pallas kernels, body(): pl.pallas_call(local_kernel, out_shape=(jax.ShapeDtypeStruct((tokens, hea...  15.4 us
    unnamed x22, local copies, waits for them, and re-layouts  10 us
    pallas_call x1, Pallas kernels, body(): pl.pallas_call(finish_kernel, out_shape=jax.ShapeDtypeStruct((n_head, tok...  9.73 us
  transfers between devices with their start and end apart: 3, of which 3 were waited for; matrix products, arithmetic and copies ran while one was open for 0% of the time, Pallas kernels for 0%

profile of v1, /device:TPU:0, one launch (start us, length us, event | category | flops | bytes accessed | tf_op | source)
XLA Modules:
  0.0 141.9 jit_solution(10987090521888341780)
XLA Ops:
  6.5 0.0 all-gather.3.cloned.1.call-start
  6.5 0.7 slice.9
  7.3 0.7 slice.10
  8.0 0.8 slice.11
  8.7 2.4 %collective-permute-start = (bf16[16,2048]{1,0:T(8,128)(2,1)S(1)}, bf16[16,2048]{1,0:T(8,128)(2,1)S(1)}, u32[]{:S(2)}, u32[]{:S(2)}) collective-permute-start(bf16[16,2048]{1,0:T(8,128)(2,1)S(1)} %pad_maximum_fusion), channel_id=1, source_target_pairs={{0,4},{4,8},{8,12},{12,16},{16,20},{20,24},{24,28},{1,5},{5,9},{9,... | collective-permute-start | bytes 196616 | tf_op jit(solution)/shard_map/ppermute | solution.py:235
  11.1 0.9 collective-permute-done.rim_ref
  12.0 0.0 copy-start.1
  12.0 1.2 copy-done.1
  13.2 0.0 copy-start.3
  13.2 1.0 copy-done.3
  14.3 0.0 copy-start.4
  14.3 1.0 copy-done.4
  15.3 0.0 copy-start.5
  15.3 0.7 copy-done.5
  16.0 0.0 copy-start.6
  16.0 0.7 copy-done.6
  16.7 0.0 copy-start.7
  16.7 0.7 copy-done.7
  17.4 0.0 copy-start.8
  17.4 0.7 copy-done.8
  18.1 0.0 copy-start.9
  18.1 0.7 copy-done.9
  18.8 15.4 %local.1 = (f32[512,1024]{1,0:T(8,128)S(1)}, bf16[512,1024]{1,0:T(8,128)(2,1)S(1)}, bf16[8,128,256]{2,1,0:T(8,128)(2,1)}) custom-call(bf16[512,512]{1,0:T(8,128)(2,1)S(1)} %copy-done.3, bf16[512,512]{1,0:T(8,128)(2,1)S(1)} %copy-done.4, bf16[512,1024]{1,0:T(8,128)(2,1)S(1)} %copy-done.1, bf16[16,2048]{1,0:T(8,128)(2,1)S(1)} %collective-permute-done.rim_ref, ...), custom_call_target="tpu_custom_call" | custom-call | tf_op jit(solution)/shard_map/local/pallas_call | solution.py:241
  34.2 0.0 copy-start
  34.2 1.4 copy-done
  35.5 0.0 all-gather.3.cloned.1.call-update
  35.5 0.0 reduce-scatter.2.cloned.1.call-start
  35.6 41.9 %all-gather.3.cloned.1.call-done = bf16[64,128,256]{2,1,0:T(8,128)(2,1)} async-done(((bf16[8,128,256]{2,1,0:T(8,128)(2,1)}), bf16[64,128,256]{2,1,0:T(8,128)(2,1)}) %all-gather.3.cloned.1.call-update) | async-done | bytes 4194320 | tf_op jit(solution)/shard_map/all_gather | solution.py:261
  77.4 0.0 copy-start.2
  77.4 1.2 copy-done.2
  78.7 0.0 copy-start.10
  78.7 0.7 copy-done.10
  79.3 9.7 %finish.1 = bf16[4,512,512]{2,1,0:T(8,128)(2,1)} custom-call(f32[512,1024]{1,0:T(8,128)} %copy-done, bf16[512,1024]{1,0:T(8,128)(2,1)S(1)} %get-tuple-element.9.qeff_ref, bf16[8,8,128,256]{3,2,1,0:T(8,128)(2,1)} %bitcast.4, bf16[512,1024]{1,0:T(8,128)(2,1)S(1)} %copy-done.2, f32[1,128]{1,0:T(1,128)S(1)} %bitcast.3, bf16[1024,2048]{1,0:T(8,128)(2,1)} %weight_ref.1), custom_call_target="tpu_custom_call" | custom-call | tf_op jit(solution)/shard_map/finish/pallas_call | solution.py:262
  89.1 0.0 reduce-scatter.2.cloned.1.call-update
  89.1 46.0 %reduce-scatter.2.cloned.1.call-done = bf16[1,512,512]{2,1,0:T(8,128)(2,1)} async-done(((bf16[4,512,512]{2,1,0:T(8,128)(2,1)}), bf16[1,512,512]{2,1,0:T(8,128)(2,1)}) %reduce-scatter.2.cloned.1.call-update) | async-done | bytes 524304 | tf_op jit(solution)/shard_map/reduce_scatter | solution.py:274
  (1 shorter events, 0.0 us)
Async XLA Ops:
  6.5 70.9 %all-gather.3.cloned.1.call-start = ((), (), s32[]{:S(2)}) async-start(), calls=%async_computation.2 | async-start | bytes 4718592 | tf_op jit(solution)/shard_map/all_gather | solution.py:261
  8.7 3.2 %collective-permute-start = (bf16[16,2048]{1,0:T(8,128)(2,1)S(1)}, bf16[16,2048]{1,0:T(8,128)(2,1)S(1)}, u32[]{:S(2)}, u32[]{:S(2)}) collective-permute-start(bf16[16,2048]{1,0:T(8,128)(2,1)S(1)} %pad_maximum_fusion), channel_id=1, source_target_pairs={{0,4},{4,8},{8,12},{12,16},{16,20},{20,24},{24,28},{1,5},{5,9},{9,... | collective-permute-start | bytes 196616 | tf_op jit(solution)/shard_map/ppermute | solution.py:235
  12.0 1.2 copy-start.1
  13.2 1.0 copy-start.3
  14.3 1.0 copy-start.4
  15.3 0.7 copy-start.5
  16.0 0.7 copy-start.6
  16.7 0.7 copy-start.7
  17.4 0.7 copy-start.8
  18.1 0.7 copy-start.9
  34.2 1.4 copy-start
  35.5 99.5 %reduce-scatter.2.cloned.1.call-start = ((), (), s32[]{:S(2)}) async-start(), calls=%async_computation.1 | async-start | bytes 2621440 | tf_op jit(solution)/shard_map/reduce_scatter | solution.py:274
  77.4 1.2 copy-start.2
  78.7 0.7 copy-start.10
Sparse Core Ops, SparseCore 0:
  35.7 41.7 all-gather.2
  89.2 45.8 reduce-scatter.1

commit v2 on v1

--- a/solution.py
+++ b/solution.py
@@ -186,41 +186,199 @@
     trans_ref[...] = st_ref[...].astype(BF16)
 
 
+def compose(later, earlier):
+    moved = mm(later[:, DV:], earlier)
+    return jnp.concatenate([moved[:, :DV] + later[:, :DV], moved[:, DV:]], 1)
+
+
 def finish_kernel(
-    out_ref, qeff_ref, every_ref, gate_ref, gain_ref, weight_ref, part_ref, start_ref, hid_ref
+    bits, n_head, steps,
+    out_ref, qeff_ref, trans_ref, gate_ref, gain_ref, weight_ref, mixed_ref,
+    start_ref, hid_ref, total_ref, prefix_ref, low_ref, give_ref, got_ref, give_b_ref, got_b_ref,
+    give_s_ref, part_ref, up_ref, down_ref,
+    state_send, state_recv, part_send, up_recv, down_recv,
 ):
-    heads = every_ref.shape[1]
+    heads = trans_ref.shape[0]
+    own = heads // 2
     tokens = out_ref.shape[0]
-    place = lax.axis_index("ctx")
-    start_ref[...] = jnp.zeros_like(start_ref)
-
-    def lap(i, unused):
-        for h in range(heads):
-            state = start_ref[h]
-            high = state.astype(BF16)
-            low = (state - high.astype(F32)).astype(BF16)
-            moved = mm(every_ref[i, h, :, DV:], jnp.concatenate([high, low], 1))
-            start_ref[h] = moved[:, :DV] + moved[:, DV:] + every_ref[i, h, :, :DV].astype(F32)
-        return unused
-
-    lax.fori_loop(0, place, lap, 0)
+    rows = tokens // steps
+    width = mixed_ref.shape[1]
+    me, z = lax.axis_index("ctx"), lax.axis_index("head")
+    core = me % 2
+    first, other = core * own, (1 - core) * own
+
+    def bit(b):
+        return (me // 2**b) % 2
+
+    def partner(b):
+        return {"ctx": me + (1 - 2 * bit(b)) * 2**b}
+
+    barrier = pltpu.get_barrier_semaphore()
+    for b in range(bits):
+        pl.semaphore_signal(
+            barrier, inc=1, device_id=partner(b), device_id_type=pl.DeviceIdType.MESH
+        )
+
+    @pl.when(z > 0)
+    def _():
+        pl.semaphore_signal(
+            barrier, inc=1, device_id={"head": z - 1}, device_id_type=pl.DeviceIdType.MESH
+        )
+
+    @pl.when(z < n_head - 1)
+    def _():
+        pl.semaphore_signal(
+            barrier, inc=1, device_id={"head": z + 1}, device_id_type=pl.DeviceIdType.MESH
+        )
+
+    inner = (z > 0) & (z < n_head - 1)
+
+    @pl.when(inner)
+    def _():
+        pl.semaphore_wait(barrier, bits + 2)
+
+    @pl.when(jnp.logical_not(inner))
+    def _():
+        pl.semaphore_wait(barrier, bits + 1)
+
+    def state_copy(b, i):
+        if b == 0:
+            src, dst = trans_ref.at[other + i], got_ref.at[0, i]
+        elif b == bits:
+            src, dst = give_s_ref.at[i], start_ref.at[first + i]
+        elif b == bits - 1:
+            src, dst = give_b_ref.at[i], got_b_ref.at[i]
+        else:
+            src, dst = give_ref.at[b, i], got_ref.at[b, i]
+        return pltpu.make_async_remote_copy(
+            src_ref=src, dst_ref=dst, send_sem=state_send.at[b, i], recv_sem=state_recv.at[b, i],
+            device_id=partner(0 if b == bits else b), device_id_type=pl.DeviceIdType.MESH,
+        )
+
+    for i in range(own):
+        state_copy(0, i).start()
+    fresh = jnp.concatenate(
+        [jnp.zeros((DK, DV), F32), (iota((DK, DK), 0) == iota((DK, DK), 1)).astype(F32)], 1
+    )
+    for i in range(own):
+        state_copy(0, i).wait_recv()
+        mine = trans_ref[first + i].astype(F32)
+        got = got_ref[0, i].astype(F32)
+        low = jnp.where(core == 0, mine, got)
+        total = compose(jnp.where(core == 0, got, mine), low)
+        low_ref[i] = low
+        total_ref[i] = total
+        prefix_ref[i] = fresh
+        if bits - 1 == 1:
+            give_b_ref[i] = total[:, :DV].astype(BF16)
+        else:
+            give_ref[1, i] = total.astype(BF16)
+        state_copy(1, i).start()
+    for b in range(1, bits - 1):
+        for i in range(own):
+            state_copy(b, i).wait_recv()
+            got = got_ref[b, i].astype(F32)
+            total = total_ref[i]
+
+            @pl.when(bit(b) == 1)
+            def _():
+                prefix_ref[i] = compose(prefix_ref[i], got)
+
+            total = compose(
+                jnp.where(bit(b) == 1, total, got), jnp.where(bit(b) == 1, got, total)
+            )
+            total_ref[i] = total
+            if b + 1 == bits - 1:
+                give_b_ref[i] = total[:, :DV].astype(BF16)
+            else:
+                give_ref[b + 1, i] = total.astype(BF16)
+            state_copy(b + 1, i).start()
+    for i in range(own):
+        state_copy(bits - 1, i).wait_recv()
+        prefix = prefix_ref[i]
+        moved = mm(prefix[:, DV:], got_b_ref[i]) + prefix[:, :DV]
+        chip = jnp.where(bit(bits - 1) == 1, moved, prefix[:, :DV])
+        low = low_ref[i]
+        later = mm(low[:, DV:], chip) + low[:, :DV]
+        start_ref[first + i] = jnp.where(core == 0, chip, later).astype(BF16)
+        give_s_ref[i] = jnp.where(core == 0, later, chip).astype(BF16)
+        state_copy(bits, i).start()
+    for i in range(own):
+        pltpu.make_async_remote_copy(
+            src_ref=give_s_ref.at[i], dst_ref=start_ref.at[other + i],
+            send_sem=state_send.at[bits, i], recv_sem=state_recv.at[bits, i],
+            device_id=partner(0), device_id_type=pl.DeviceIdType.MESH,
+        ).wait_recv()
+
+    def part_copy(up, d, c):
+        at = pl.ds(c * rows, rows)
+        return pltpu.make_async_remote_copy(
+            src_ref=part_ref.at[d, at], dst_ref=(up_ref if up else down_ref).at[d, at],
+            send_sem=part_send.at[d, c], recv_sem=(up_recv if up else down_recv).at[d, c],
+            device_id={"head": z + 1 if up else z - 1}, device_id_type=pl.DeviceIdType.MESH,
+        )
+
     gain = gain_ref[...]
-    rows = 128
-
-    def chunk(c, unused):
-        at = pl.ds(pl.multiple_of(c * rows, rows), rows)
+    for c in range(steps):
+        at = slice(c * rows, (c + 1) * rows)
         for h in range(heads):
             cs = slice(h * DV, (h + 1) * DV)
             o = out_ref[at, cs] + mm(qeff_ref[at, cs], start_ref[h])
             n = o * lax.rsqrt(jnp.mean(o * o, -1, keepdims=True) + 1e-06)
             hid_ref[at, cs] = (n * gain * silu(gate_ref[at, cs].astype(F32))).astype(BF16)
         hidden = hid_ref[at, :]
-        width = part_ref.shape[2]
-        for d in range(part_ref.shape[0]):
+        for d in range(n_head):
             part_ref[d, at, :] = mm(hidden, weight_ref[:, d * width : (d + 1) * width]).astype(BF16)
-        return unused
-
-    lax.fori_loop(0, tokens // rows, chunk, 0)
+
+        @pl.when(z == 0)
+        def _():
+            for d in range(n_head - 1, 0, -1):
+                part_copy(True, d, c).start()
+
+        @pl.when(z == n_head - 1)
+        def _():
+            for d in range(n_head - 1):
+                part_copy(False, d, c).start()
+
+    def pass_on(up, d, c):
+        inside = (z > 0) & (z < d) if up else (z < n_head - 1) & (z > d)
+
+        @pl.when(inside)
+        def _():
+            part_copy(up, d, c).wait_recv()
+            at = slice(c * rows, (c + 1) * rows)
+            landed = (up_ref if up else down_ref)[d, at, :].astype(F32)
+            part_ref[d, at, :] = (part_ref[d, at, :].astype(F32) + landed).astype(BF16)
+            part_copy(up, d, c).start()
+
+    for c in range(steps):
+        for d in range(n_head - 1, 0, -1):
+            pass_on(True, d, c)
+            pass_on(False, n_head - 1 - d, c)
+    for c in range(steps):
+        at = slice(c * rows, (c + 1) * rows)
+        for d in range(n_head):
+
+            @pl.when(z == d)
+            def _():
+                total = part_ref[d, at, :].astype(F32)
+                if d > 0:
+                    part_copy(True, d, c).wait_recv()
+                    total = total + up_ref[d, at, :].astype(F32)
+                if d < n_head - 1:
+                    part_copy(False, d, c).wait_recv()
+                    total = total + down_ref[d, at, :].astype(F32)
+                mixed_ref[at, :] = total.astype(BF16)
+
+    for b in range(bits + 1):
+        for i in range(own):
+            state_copy(b, i).wait_send()
+    for c in range(steps):
+        for d in range(n_head):
+
+            @pl.when(z != d)
+            def _():
+                part_copy(True, d, c).wait_send()
 
 
 def body(
@@ -258,20 +416,43 @@
         query_raw, key_raw, value_raw, rim, conv_query, conv_key, conv_value,
         decay_log, write_beta,
     )
-    every = lax.all_gather(trans, "ctx")
-    part = pl.pallas_call(
-        finish_kernel,
-        out_shape=jax.ShapeDtypeStruct((n_head, tokens, out_weight.shape[1] // n_head), BF16),
+    bits = n_ctx.bit_length() - 1
+    assert n_ctx == 2**bits and bits > 1
+    own = heads // 2
+    steps = 4
+    features = out_weight.shape[1] // n_head
+    parts = pltpu.VMEM((n_head, tokens, features), BF16)
+    state = pltpu.VMEM((own, DK, DV + DK), F32)
+    return pl.pallas_call(
+        functools.partial(finish_kernel, bits, n_head, steps),
+        out_shape=jax.ShapeDtypeStruct((tokens, features), BF16),
         in_specs=[vmem] * 6,
         out_specs=vmem,
         scratch_shapes=[
-            pltpu.VMEM((heads, DK, DV), F32),
+            pltpu.VMEM((heads, DK, DV), BF16),
             pltpu.VMEM((tokens, heads * DV), BF16),
+            state,
+            state,
+            state,
+            pltpu.VMEM((bits, own, DK, DV + DK), BF16),
+            pltpu.VMEM((bits, own, DK, DV + DK), BF16),
+            pltpu.VMEM((own, DK, DV), BF16),
+            pltpu.VMEM((own, DK, DV), BF16),
+            pltpu.VMEM((own, DK, DV), BF16),
+            parts,
+            parts,
+            parts,
+            pltpu.SemaphoreType.DMA((bits + 1, own)),
+            pltpu.SemaphoreType.DMA((bits + 1, own)),
+            pltpu.SemaphoreType.DMA((n_head, steps)),
+            pltpu.SemaphoreType.DMA((n_head, steps)),
+            pltpu.SemaphoreType.DMA((n_head, steps)),
         ],
-        compiler_params=pltpu.CompilerParams(vmem_limit_bytes=48 * 2**20),
+        compiler_params=pltpu.CompilerParams(
+            vmem_limit_bytes=48 * 2**20, collective_id=0, has_side_effects=True
+        ),
         name="finish",
-    )(out, qeff, every, gate_input, norm_gain.reshape(1, DV), out_weight)
-    return lax.psum_scatter(part, "head", scatter_dimension=0)
+    )(out, qeff, trans, gate_input, norm_gain.reshape(1, DV), out_weight)
 
 
 def solution(mesh):

time: 143 us -> 102 us (0.71)
  waiting for transfers between devices: 88.7 us -> 0.88 us
  Pallas kernels: 25.1 us -> 86.3 us
  between operations: 13.4 us -> 0.05 us
    pallas_call x1, Pallas kernels: 9.73 us -> 71.8 us  [body(): pl.pallas_call(functools.partial(finish_kernel, bits, n_head, steps), out...]
    reduce_scatter x1 -> x0, waiting for transfers between devices: 46 us -> none  [body(): return lax.psum_scatter(part, 'head', scatter_dimension=0)]
    all_gather x1 -> x0, waiting for transfers between devices: 41.9 us -> none  [body(): every = lax.all_gather(trans, 'ctx')]
    unnamed x22 -> x21, local copies, waits for them, and re-layouts: 10 us -> 9.48 us
  transfers between devices with their start and end apart: 3 -> 1, of which waited for: 3 -> 1; matrix products, arithmetic and copies ran while one was open for 0% -> 0% of each run, Pallas kernels for 0% -> 0%
where the time goes in v2:
time: 102 us; the launch traced here: 101 us
  Pallas kernels  86.3 us (85%)
  local copies, waits for them, and re-layouts  11.7 us (11%)
  starting transfers between devices  2.36 us (2%)
    pallas_call x1, Pallas kernels, body(): pl.pallas_call(functools.partial(finish_kernel, bits, n_head, steps), out...  71.8 us
    pallas_call x1, Pallas kernels, body(): pl.pallas_call(local_kernel, out_shape=(jax.ShapeDtypeStruct((tokens, hea...  14.6 us
    unnamed x21, local copies, waits for them, and re-layouts  9.48 us
    ppermute x1, starting transfers between devices, body(): lax.ppermute(jnp.concatenate([x[tokens - RIM:] for x in (query_raw, key_r...  2.36 us
    slice x3, local copies, waits for them, and re-layouts, body(): x[tokens - RIM:]  2.2 us
  transfers between devices with their start and end apart: 1, of which 1 were waited for; matrix products, arithmetic and copies ran while one was open for 0% of the time, Pallas kernels for 0%

profile of v2, /device:TPU:0, one launch (start us, length us, event | category | flops | bytes accessed | tf_op | source)
XLA Modules:
  0.0 101.3 jit_solution(5750284870222524470)
XLA Ops:
  0.0 0.7 slice.9
  0.7 0.7 slice.10
  1.4 0.8 slice.11
  2.2 2.4 %collective-permute-start = (bf16[16,2048]{1,0:T(8,128)(2,1)S(1)}, bf16[16,2048]{1,0:T(8,128)(2,1)S(1)}, u32[]{:S(2)}, u32[]{:S(2)}) collective-permute-start(bf16[16,2048]{1,0:T(8,128)(2,1)S(1)} %pad_maximum_fusion), channel_id=1, source_target_pairs={{0,4},{4,8},{8,12},{12,16},{16,20},{20,24},{24,28},{1,5},{5,9},{9,... | collective-permute-start | bytes 196616 | tf_op jit(solution)/shard_map/ppermute | solution.py:393
  4.6 0.9 collective-permute-done.rim_ref
  5.4 0.0 copy-start
  5.5 1.2 %copy-done = bf16[512,1024]{1,0:T(8,128)(2,1)S(1)} copy-done((bf16[512,1024]{1,0:T(8,128)(2,1)S(1)}, bf16[512,1024]{1,0:T(8,128)(2,1)}, u32[]{:S(2)}) %copy-start) | copy-done | bytes 1048600
  6.7 0.0 copy-start.2
  6.7 1.0 %copy-done.2 = bf16[512,512]{1,0:T(8,128)(2,1)S(1)} copy-done((bf16[512,512]{1,0:T(8,128)(2,1)S(1)}, bf16[512,512]{1,0:T(8,128)(2,1)}, u32[]{:S(2)}) %copy-start.2) | copy-done | bytes 524312
  7.7 0.0 copy-start.3
  7.7 1.0 %copy-done.3 = bf16[512,512]{1,0:T(8,128)(2,1)S(1)} copy-done((bf16[512,512]{1,0:T(8,128)(2,1)S(1)}, bf16[512,512]{1,0:T(8,128)(2,1)}, u32[]{:S(2)}) %copy-start.3) | copy-done | bytes 524312
  8.8 0.0 copy-start.4
  8.8 0.7 copy-done.4
  9.5 0.0 copy-start.5
  9.5 0.7 copy-done.5
  10.2 0.0 copy-start.6
  10.2 0.7 copy-done.6
  10.9 0.0 copy-start.7
  10.9 0.7 copy-done.7
  11.6 0.0 copy-start.8
  11.6 0.7 copy-done.8
  12.3 14.6 %local.1 = (f32[512,1024]{1,0:T(8,128)S(1)}, bf16[512,1024]{1,0:T(8,128)(2,1)S(1)}, bf16[8,128,256]{2,1,0:T(8,128)(2,1)S(1)}) custom-call(bf16[512,512]{1,0:T(8,128)(2,1)S(1)} %copy-done.2, bf16[512,512]{1,0:T(8,128)(2,1)S(1)} %copy-done.3, bf16[512,1024]{1,0:T(8,128)(2,1)S(1)} %copy-done, bf16[16,2048]{1,0:T(8,128)(2,1)S(1)} %collective-permute-done.rim_ref, ...), custom_call_target="tpu_custom_call" | custom-call | tf_op jit(solution)/shard_map/local/pallas_call | solution.py:399
  26.8 0.0 copy-start.1
  26.8 1.2 %copy-done.1 = bf16[512,1024]{1,0:T(8,128)(2,1)S(1)} copy-done((bf16[512,1024]{1,0:T(8,128)(2,1)S(1)}, bf16[512,1024]{1,0:T(8,128)(2,1)}, u32[]{:S(2)}) %copy-start.1) | copy-done | bytes 1048600
  28.1 0.0 copy-start.9
  28.1 0.7 copy-done.9
  28.7 71.8 %finish.1 = bf16[512,512]{1,0:T(8,128)(2,1)S(1)} custom-call(f32[512,1024]{1,0:T(8,128)S(1)} %get-tuple-element.8.out_ref, bf16[512,1024]{1,0:T(8,128)(2,1)S(1)} %get-tuple-element.9.qeff_ref, bf16[8,128,256]{2,1,0:T(8,128)(2,1)S(1)} %get-tuple-element.10.trans_ref, bf16[512,1024]{1,0:T(8,128)(2,1)S(1)} %copy-done.1, f32[1,128]{1,0:T(1,128)S(1)} %bitcast.1, ...), custom_call_target="tpu_custom_call" | custom-call | tf_op jit(solution)/shard_map/finish/pallas_call | solution.py:426
  100.5 0.8 copy.13
  (1 shorter events, 0.0 us)
Async XLA Ops:
  2.2 3.2 %collective-permute-start = (bf16[16,2048]{1,0:T(8,128)(2,1)S(1)}, bf16[16,2048]{1,0:T(8,128)(2,1)S(1)}, u32[]{:S(2)}, u32[]{:S(2)}) collective-permute-start(bf16[16,2048]{1,0:T(8,128)(2,1)S(1)} %pad_maximum_fusion), channel_id=1, source_target_pairs={{0,4},{4,8},{8,12},{12,16},{16,20},{20,24},{24,28},{1,5},{5,9},{9,... | collective-permute-start | bytes 196616 | tf_op jit(solution)/shard_map/ppermute | solution.py:393
  5.4 1.2 %copy-start = (bf16[512,1024]{1,0:T(8,128)(2,1)S(1)}, bf16[512,1024]{1,0:T(8,128)(2,1)}, u32[]{:S(2)}) copy-start(bf16[512,1024]{1,0:T(8,128)(2,1)} %v_ref.1) | copy-start | bytes 3145732
  6.7 1.0 %copy-start.2 = (bf16[512,512]{1,0:T(8,128)(2,1)S(1)}, bf16[512,512]{1,0:T(8,128)(2,1)}, u32[]{:S(2)}) copy-start(bf16[512,512]{1,0:T(8,128)(2,1)} %q_ref.1) | copy-start | bytes 1572868
  7.7 1.0 %copy-start.3 = (bf16[512,512]{1,0:T(8,128)(2,1)S(1)}, bf16[512,512]{1,0:T(8,128)(2,1)}, u32[]{:S(2)}) copy-start(bf16[512,512]{1,0:T(8,128)(2,1)} %k_ref.1) | copy-start | bytes 1572868
  8.8 0.7 copy-start.4
  9.5 0.7 copy-start.5
  10.2 0.7 copy-start.6
  10.9 0.7 copy-start.7
  11.6 0.7 copy-start.8
  26.8 1.2 %copy-start.1 = (bf16[512,1024]{1,0:T(8,128)(2,1)S(1)}, bf16[512,1024]{1,0:T(8,128)(2,1)}, u32[]{:S(2)}) copy-start(bf16[512,1024]{1,0:T(8,128)(2,1)} %gate_ref.1) | copy-start | bytes 3145732
  28.1 0.7 copy-start.9

commit v3 on v2

--- a/solution.py
+++ b/solution.py
@@ -403,7 +403,14 @@
             jax.ShapeDtypeStruct((tokens, heads * DK), BF16),
             jax.ShapeDtypeStruct((heads, DK, DV + DK), BF16),
         ),
-        in_specs=[vmem] * 9,
+        grid=(1,),
+        in_specs=[
+            pl.BlockSpec(x.shape, lambda i: (0, 0))
+            for x in (
+                query_raw, key_raw, value_raw, rim, conv_query, conv_key, conv_value,
+                decay_log, write_beta,
+            )
+        ],
         out_specs=[vmem] * 3,
         scratch_shapes=[
             pltpu.VMEM((8, channels), F32),

time: 102 us -> 102 us (level)
  no operation moved by 1% of the time
where the time goes in v3:
time: 102 us; the launch traced here: 101 us
  Pallas kernels  86.3 us (85%)
  local copies, waits for them, and re-layouts  11.7 us (11%)
  starting transfers between devices  2.36 us (2%)
    pallas_call x1, Pallas kernels, body(): pl.pallas_call(functools.partial(finish_kernel, bits, n_head, steps), out...  71.8 us
    pallas_call x1, Pallas kernels, body(): pl.pallas_call(local_kernel, out_shape=(jax.ShapeDtypeStruct((tokens, hea...  14.6 us
    unnamed x21, local copies, waits for them, and re-layouts  9.48 us
    ppermute x1, starting transfers between devices, body(): lax.ppermute(jnp.concatenate([x[tokens - RIM:] for x in (query_raw, key_r...  2.36 us
    slice x3, local copies, waits for them, and re-layouts, body(): x[tokens - RIM:]  2.2 us
  transfers between devices with their start and end apart: 1, of which 1 were waited for; matrix products, arithmetic and copies ran while one was open for 0% of the time, Pallas kernels for 0%

profile of v3, /device:TPU:0, one launch (start us, length us, event | category | flops | bytes accessed | tf_op | source)
XLA Modules:
  0.0 101.3 jit_solution(5750284870222524470)
XLA Ops:
  0.0 0.7 slice.9
  0.7 0.7 slice.10
  1.4 0.8 slice.11
  2.2 2.4 %collective-permute-start = (bf16[16,2048]{1,0:T(8,128)(2,1)S(1)}, bf16[16,2048]{1,0:T(8,128)(2,1)S(1)}, u32[]{:S(2)}, u32[]{:S(2)}) collective-permute-start(bf16[16,2048]{1,0:T(8,128)(2,1)S(1)} %pad_maximum_fusion), channel_id=1, source_target_pairs={{0,4},{4,8},{8,12},{12,16},{16,20},{20,24},{24,28},{1,5},{5,9},{9,... | collective-permute-start | bytes 196616 | tf_op jit(solution)/shard_map/ppermute | solution.py:393
  4.6 0.9 collective-permute-done.rim_ref
  5.4 0.0 copy-start
  5.5 1.2 %copy-done = bf16[512,1024]{1,0:T(8,128)(2,1)S(1)} copy-done((bf16[512,1024]{1,0:T(8,128)(2,1)S(1)}, bf16[512,1024]{1,0:T(8,128)(2,1)}, u32[]{:S(2)}) %copy-start) | copy-done | bytes 1048600
  6.7 0.0 copy-start.2
  6.7 1.0 %copy-done.2 = bf16[512,512]{1,0:T(8,128)(2,1)S(1)} copy-done((bf16[512,512]{1,0:T(8,128)(2,1)S(1)}, bf16[512,512]{1,0:T(8,128)(2,1)}, u32[]{:S(2)}) %copy-start.2) | copy-done | bytes 524312
  7.7 0.0 copy-start.3
  7.7 1.0 %copy-done.3 = bf16[512,512]{1,0:T(8,128)(2,1)S(1)} copy-done((bf16[512,512]{1,0:T(8,128)(2,1)S(1)}, bf16[512,512]{1,0:T(8,128)(2,1)}, u32[]{:S(2)}) %copy-start.3) | copy-done | bytes 524312
  8.8 0.0 copy-start.4
  8.8 0.7 copy-done.4
  9.5 0.0 copy-start.5
  9.5 0.7 copy-done.5
  10.2 0.0 copy-start.6
  10.2 0.7 copy-done.6
  10.9 0.0 copy-start.7
  10.9 0.7 copy-done.7
  11.6 0.0 copy-start.8
  11.6 0.7 copy-done.8
  12.3 14.6 %local.1 = (f32[512,1024]{1,0:T(8,128)S(1)}, bf16[512,1024]{1,0:T(8,128)(2,1)S(1)}, bf16[8,128,256]{2,1,0:T(8,128)(2,1)S(1)}) custom-call(bf16[512,512]{1,0:T(8,128)(2,1)S(1)} %copy-done.2, bf16[512,512]{1,0:T(8,128)(2,1)S(1)} %copy-done.3, bf16[512,1024]{1,0:T(8,128)(2,1)S(1)} %copy-done, bf16[16,2048]{1,0:T(8,128)(2,1)S(1)} %collective-permute-done.rim_ref, ...), custom_call_target="tpu_custom_call" | custom-call | tf_op jit(solution)/shard_map/local/pallas_call | solution.py:399
  26.8 0.0 copy-start.1
  26.8 1.2 %copy-done.1 = bf16[512,1024]{1,0:T(8,128)(2,1)S(1)} copy-done((bf16[512,1024]{1,0:T(8,128)(2,1)S(1)}, bf16[512,1024]{1,0:T(8,128)(2,1)}, u32[]{:S(2)}) %copy-start.1) | copy-done | bytes 1048600
  28.1 0.0 copy-start.9
  28.1 0.7 copy-done.9
  28.7 71.8 %finish.1 = bf16[512,512]{1,0:T(8,128)(2,1)S(1)} custom-call(f32[512,1024]{1,0:T(8,128)S(1)} %get-tuple-element.8.out_ref, bf16[512,1024]{1,0:T(8,128)(2,1)S(1)} %get-tuple-element.9.qeff_ref, bf16[8,128,256]{2,1,0:T(8,128)(2,1)S(1)} %get-tuple-element.10.trans_ref, bf16[512,1024]{1,0:T(8,128)(2,1)S(1)} %copy-done.1, f32[1,128]{1,0:T(1,128)S(1)} %bitcast.1, ...), custom_call_target="tpu_custom_call" | custom-call | tf_op jit(solution)/shard_map/finish/pallas_call | solution.py:433
  100.5 0.8 copy.13
  (1 shorter events, 0.0 us)
Async XLA Ops:
  2.2 3.2 %collective-permute-start = (bf16[16,2048]{1,0:T(8,128)(2,1)S(1)}, bf16[16,2048]{1,0:T(8,128)(2,1)S(1)}, u32[]{:S(2)}, u32[]{:S(2)}) collective-permute-start(bf16[16,2048]{1,0:T(8,128)(2,1)S(1)} %pad_maximum_fusion), channel_id=1, source_target_pairs={{0,4},{4,8},{8,12},{12,16},{16,20},{20,24},{24,28},{1,5},{5,9},{9,... | collective-permute-start | bytes 196616 | tf_op jit(solution)/shard_map/ppermute | solution.py:393
  5.4 1.2 %copy-start = (bf16[512,1024]{1,0:T(8,128)(2,1)S(1)}, bf16[512,1024]{1,0:T(8,128)(2,1)}, u32[]{:S(2)}) copy-start(bf16[512,1024]{1,0:T(8,128)(2,1)} %v_ref.1) | copy-start | bytes 3145732
  6.7 1.0 %copy-start.2 = (bf16[512,512]{1,0:T(8,128)(2,1)S(1)}, bf16[512,512]{1,0:T(8,128)(2,1)}, u32[]{:S(2)}) copy-start(bf16[512,512]{1,0:T(8,128)(2,1)} %q_ref.1) | copy-start | bytes 1572868
  7.7 1.0 %copy-start.3 = (bf16[512,512]{1,0:T(8,128)(2,1)S(1)}, bf16[512,512]{1,0:T(8,128)(2,1)}, u32[]{:S(2)}) copy-start(bf16[512,512]{1,0:T(8,128)(2,1)} %k_ref.1) | copy-start | bytes 1572868
  8.8 0.7 copy-start.4
  9.5 0.7 copy-start.5
  10.2 0.7 copy-start.6
  10.9 0.7 copy-start.7
  11.6 0.7 copy-start.8
  26.8 1.2 %copy-start.1 = (bf16[512,1024]{1,0:T(8,128)(2,1)S(1)}, bf16[512,1024]{1,0:T(8,128)(2,1)}, u32[]{:S(2)}) copy-start(bf16[512,1024]{1,0:T(8,128)(2,1)} %gate_ref.1) | copy-start | bytes 3145732
  28.1 0.7 copy-start.9

commit v4 on v3

--- a/solution.py
+++ b/solution.py
@@ -202,6 +202,7 @@
     own = heads // 2
     tokens = out_ref.shape[0]
     rows = tokens // steps
+    group = 2
     width = mixed_ref.shape[1]
     me, z = lax.axis_index("ctx"), lax.axis_index("head")
     core = me % 2
@@ -310,8 +311,11 @@
             device_id=partner(0), device_id_type=pl.DeviceIdType.MESH,
         ).wait_recv()
 
+    def piece(c):
+        return pl.ds(pl.multiple_of(c * rows, rows), rows)
+
     def part_copy(up, d, c):
-        at = pl.ds(c * rows, rows)
+        at = piece(c)
         return pltpu.make_async_remote_copy(
             src_ref=part_ref.at[d, at], dst_ref=(up_ref if up else down_ref).at[d, at],
             send_sem=part_send.at[d, c], recv_sem=(up_recv if up else down_recv).at[d, c],
@@ -319,8 +323,8 @@
         )
 
     gain = gain_ref[...]
-    for c in range(steps):
-        at = slice(c * rows, (c + 1) * rows)
+    for t in range(steps // group):
+        at = slice(t * group * rows, (t + 1) * group * rows)
         for h in range(heads):
             cs = slice(h * DV, (h + 1) * DV)
             o = out_ref[at, cs] + mm(qeff_ref[at, cs], start_ref[h])
@@ -330,15 +334,20 @@
         for d in range(n_head):
             part_ref[d, at, :] = mm(hidden, weight_ref[:, d * width : (d + 1) * width]).astype(BF16)
 
+        def feed(up, targets):
+            for c in range(t * group, (t + 1) * group):
+                for d in targets:
+                    if c > 0:
+                        part_copy(up, d, c - 1).wait_send()
+                    part_copy(up, d, c).start()
+
         @pl.when(z == 0)
         def _():
-            for d in range(n_head - 1, 0, -1):
-                part_copy(True, d, c).start()
+            feed(True, range(n_head - 1, 0, -1))
 
         @pl.when(z == n_head - 1)
         def _():
-            for d in range(n_head - 1):
-                part_copy(False, d, c).start()
+            feed(False, range(n_head - 1))
 
     def pass_on(up, d, c):
         inside = (z > 0) & (z < d) if up else (z < n_head - 1) & (z > d)
@@ -346,37 +355,64 @@
         @pl.when(inside)
         def _():
             part_copy(up, d, c).wait_recv()
-            at = slice(c * rows, (c + 1) * rows)
-            landed = (up_ref if up else down_ref)[d, at, :].astype(F32)
-            part_ref[d, at, :] = (part_ref[d, at, :].astype(F32) + landed).astype(BF16)
+            landed = (up_ref if up else down_ref)[d, piece(c), :].astype(F32)
+            part_ref[d, piece(c), :] = (part_ref[d, piece(c), :].astype(F32) + landed).astype(BF16)
             part_copy(up, d, c).start()
 
-    for c in range(steps):
+    def ups(c):
         for d in range(n_head - 1, 0, -1):
             pass_on(True, d, c)
-            pass_on(False, n_head - 1 - d, c)
-    for c in range(steps):
-        at = slice(c * rows, (c + 1) * rows)
+
+    def downs(c):
+        for d in range(n_head - 1):
+            pass_on(False, d, c)
+
+    @pl.when(z < n_head // 2)
+    def _():
+        def lap(c, unused):
+            ups(c)
+            downs(c)
+            return unused
+
+        lax.fori_loop(0, steps, lap, 0)
+
+    @pl.when(z >= n_head // 2)
+    def _():
+        def lap(c, unused):
+            downs(c)
+            ups(c)
+            return unused
+
+        lax.fori_loop(0, steps, lap, 0)
+
+    def close(c, unused):
         for d in range(n_head):
 
             @pl.when(z == d)
             def _():
-                total = part_ref[d, at, :].astype(F32)
+                total = part_ref[d, piece(c), :].astype(F32)
                 if d > 0:
                     part_copy(True, d, c).wait_recv()
-                    total = total + up_ref[d, at, :].astype(F32)
+                    total = total + up_ref[d, piece(c), :].astype(F32)
                 if d < n_head - 1:
                     part_copy(False, d, c).wait_recv()
-                    total = total + down_ref[d, at, :].astype(F32)
-                mixed_ref[at, :] = total.astype(BF16)
+                    total = total + down_ref[d, piece(c), :].astype(F32)
+                mixed_ref[piece(c), :] = total.astype(BF16)
+
+        return unused
+
+    lax.fori_loop(0, steps, close, 0)
 
     for b in range(bits + 1):
         for i in range(own):
             state_copy(b, i).wait_send()
     for c in range(steps):
         for d in range(n_head):
-
-            @pl.when(z != d)
+            unsent = z != d
+            if c < steps - 1:
+                unsent = unsent & (z > 0) & (z < n_head - 1)
+
+            @pl.when(unsent)
             def _():
                 part_copy(True, d, c).wait_send()
 
@@ -426,7 +462,7 @@
     bits = n_ctx.bit_length() - 1
     assert n_ctx == 2**bits and bits > 1
     own = heads // 2
-    steps = 4
+    steps = 8
     features = out_weight.shape[1] // n_head
     parts = pltpu.VMEM((n_head, tokens, features), BF16)
     state = pltpu.VMEM((own, DK, DV + DK), F32)

time: 102 us -> 94.5 us (0.926)
  Pallas kernels: 86.3 us -> 78.8 us
    pallas_call x1, Pallas kernels: 71.8 us -> 64.3 us  [body(): pl.pallas_call(functools.partial(finish_kernel, bits, n_head, steps), out...]
where the time goes in v4:
time: 94.5 us; the launch traced here: 93.8 us
  Pallas kernels  78.8 us (83%)
  local copies, waits for them, and re-layouts  11.7 us (12%)
  starting transfers between devices  2.36 us (2%)
    pallas_call x1, Pallas kernels, body(): pl.pallas_call(functools.partial(finish_kernel, bits, n_head, steps), out...  64.3 us
    pallas_call x1, Pallas kernels, body(): pl.pallas_call(local_kernel, out_shape=(jax.ShapeDtypeStruct((tokens, hea...  14.6 us
    unnamed x21, local copies, waits for them, and re-layouts  9.48 us
    ppermute x1, starting transfers between devices, body(): lax.ppermute(jnp.concatenate([x[tokens - RIM:] for x in (query_raw, key_r...  2.36 us
    slice x3, local copies, waits for them, and re-layouts, body(): x[tokens - RIM:]  2.2 us
  transfers between devices with their start and end apart: 1, of which 1 were waited for; matrix products, arithmetic and copies ran while one was open for 0% of the time, Pallas kernels for 0%

profile of v4, /device:TPU:0, one launch (start us, length us, event | category | flops | bytes accessed | tf_op | source)
XLA Modules:
  0.0 93.8 jit_solution(16178720608024035019)
XLA Ops:
  0.0 0.7 slice.9
  0.7 0.7 slice.10
  1.4 0.8 slice.11
  2.2 2.4 %collective-permute-start = (bf16[16,2048]{1,0:T(8,128)(2,1)S(1)}, bf16[16,2048]{1,0:T(8,128)(2,1)S(1)}, u32[]{:S(2)}, u32[]{:S(2)}) collective-permute-start(bf16[16,2048]{1,0:T(8,128)(2,1)S(1)} %pad_maximum_fusion), channel_id=1, source_target_pairs={{0,4},{4,8},{8,12},{12,16},{16,20},{20,24},{24,28},{1,5},{5,9},{9,... | collective-permute-start | bytes 196616 | tf_op jit(solution)/shard_map/ppermute | solution.py:429
  4.6 0.9 collective-permute-done.rim_ref
  5.4 0.0 copy-start
  5.5 1.2 %copy-done = bf16[512,1024]{1,0:T(8,128)(2,1)S(1)} copy-done((bf16[512,1024]{1,0:T(8,128)(2,1)S(1)}, bf16[512,1024]{1,0:T(8,128)(2,1)}, u32[]{:S(2)}) %copy-start) | copy-done | bytes 1048600
  6.7 0.0 copy-start.2
  6.7 1.0 %copy-done.2 = bf16[512,512]{1,0:T(8,128)(2,1)S(1)} copy-done((bf16[512,512]{1,0:T(8,128)(2,1)S(1)}, bf16[512,512]{1,0:T(8,128)(2,1)}, u32[]{:S(2)}) %copy-start.2) | copy-done | bytes 524312
  7.7 0.0 copy-start.3
  7.7 1.0 %copy-done.3 = bf16[512,512]{1,0:T(8,128)(2,1)S(1)} copy-done((bf16[512,512]{1,0:T(8,128)(2,1)S(1)}, bf16[512,512]{1,0:T(8,128)(2,1)}, u32[]{:S(2)}) %copy-start.3) | copy-done | bytes 524312
  8.8 0.0 copy-start.4
  8.8 0.7 copy-done.4
  9.5 0.0 copy-start.5
  9.5 0.7 copy-done.5
  10.2 0.0 copy-start.6
  10.2 0.7 copy-done.6
  10.9 0.0 copy-start.7
  10.9 0.7 copy-done.7
  11.6 0.0 copy-start.8
  11.6 0.7 copy-done.8
  12.3 14.6 %local.1 = (f32[512,1024]{1,0:T(8,128)S(1)}, bf16[512,1024]{1,0:T(8,128)(2,1)S(1)}, bf16[8,128,256]{2,1,0:T(8,128)(2,1)S(1)}) custom-call(bf16[512,512]{1,0:T(8,128)(2,1)S(1)} %copy-done.2, bf16[512,512]{1,0:T(8,128)(2,1)S(1)} %copy-done.3, bf16[512,1024]{1,0:T(8,128)(2,1)S(1)} %copy-done, bf16[16,2048]{1,0:T(8,128)(2,1)S(1)} %collective-permute-done.rim_ref, ...), custom_call_target="tpu_custom_call" | custom-call | tf_op jit(solution)/shard_map/local/pallas_call | solution.py:435
  26.8 0.0 copy-start.1
  26.8 1.2 %copy-done.1 = bf16[512,1024]{1,0:T(8,128)(2,1)S(1)} copy-done((bf16[512,1024]{1,0:T(8,128)(2,1)S(1)}, bf16[512,1024]{1,0:T(8,128)(2,1)}, u32[]{:S(2)}) %copy-start.1) | copy-done | bytes 1048600
  28.1 0.0 copy-start.9
  28.1 0.7 copy-done.9
  28.7 64.3 %finish.1 = bf16[512,512]{1,0:T(8,128)(2,1)S(1)} custom-call(f32[512,1024]{1,0:T(8,128)S(1)} %get-tuple-element.8.out_ref, bf16[512,1024]{1,0:T(8,128)(2,1)S(1)} %get-tuple-element.9.qeff_ref, bf16[8,128,256]{2,1,0:T(8,128)(2,1)S(1)} %get-tuple-element.10.trans_ref, bf16[512,1024]{1,0:T(8,128)(2,1)S(1)} %copy-done.1, f32[1,128]{1,0:T(1,128)S(1)} %bitcast.1, ...), custom_call_target="tpu_custom_call" | custom-call | tf_op jit(solution)/shard_map/finish/pallas_call | solution.py:469
  93.0 0.8 copy.13
  (1 shorter events, 0.0 us)
Async XLA Ops:
  2.2 3.2 %collective-permute-start = (bf16[16,2048]{1,0:T(8,128)(2,1)S(1)}, bf16[16,2048]{1,0:T(8,128)(2,1)S(1)}, u32[]{:S(2)}, u32[]{:S(2)}) collective-permute-start(bf16[16,2048]{1,0:T(8,128)(2,1)S(1)} %pad_maximum_fusion), channel_id=1, source_target_pairs={{0,4},{4,8},{8,12},{12,16},{16,20},{20,24},{24,28},{1,5},{5,9},{9,... | collective-permute-start | bytes 196616 | tf_op jit(solution)/shard_map/ppermute | solution.py:429
  5.4 1.2 %copy-start = (bf16[512,1024]{1,0:T(8,128)(2,1)S(1)}, bf16[512,1024]{1,0:T(8,128)(2,1)}, u32[]{:S(2)}) copy-start(bf16[512,1024]{1,0:T(8,128)(2,1)} %v_ref.1) | copy-start | bytes 3145732
  6.7 1.0 %copy-start.2 = (bf16[512,512]{1,0:T(8,128)(2,1)S(1)}, bf16[512,512]{1,0:T(8,128)(2,1)}, u32[]{:S(2)}) copy-start(bf16[512,512]{1,0:T(8,128)(2,1)} %q_ref.1) | copy-start | bytes 1572868
  7.7 1.0 %copy-start.3 = (bf16[512,512]{1,0:T(8,128)(2,1)S(1)}, bf16[512,512]{1,0:T(8,128)(2,1)}, u32[]{:S(2)}) copy-start(bf16[512,512]{1,0:T(8,128)(2,1)} %k_ref.1) | copy-start | bytes 1572868
  8.8 0.7 copy-start.4
  9.5 0.7 copy-start.5
  10.2 0.7 copy-start.6
  10.9 0.7 copy-start.7
  11.6 0.7 copy-start.8
  26.8 1.2 %copy-start.1 = (bf16[512,1024]{1,0:T(8,128)(2,1)S(1)}, bf16[512,1024]{1,0:T(8,128)(2,1)}, u32[]{:S(2)}) copy-start(bf16[512,1024]{1,0:T(8,128)(2,1)} %gate_ref.1) | copy-start | bytes 3145732
  28.1 0.7 copy-start.9

commit v5 on v4

--- a/solution.py
+++ b/solution.py
@@ -186,6 +186,25 @@
     trans_ref[...] = st_ref[...].astype(BF16)
 
 
+def local_entry(
+    q_ref, k_ref, v_ref, dec_ref, beta_ref, rim_ref, taps_ref,
+    out_ref, qeff_ref, trans_ref,
+    tail_ref, bd_ref, st_ref, q_in, k_in, v_in, dec_in, beta_in, sem,
+):
+    pairs = ((q_ref, q_in), (k_ref, k_in), (v_ref, v_in), (dec_ref, dec_in), (beta_ref, beta_in))
+    copies = [pltpu.make_async_copy(a, b, sem.at[i]) for i, (a, b) in enumerate(pairs)]
+    for copy in copies:
+        copy.start()
+    for copy in copies:
+        copy.wait()
+    qc, kc = q_ref.shape[1], k_ref.shape[1]
+    local_kernel(
+        q_in, k_in, v_in, rim_ref,
+        taps_ref.at[:, :qc], taps_ref.at[:, qc : qc + kc], taps_ref.at[:, qc + kc :],
+        dec_in, beta_in, out_ref, qeff_ref, trans_ref, tail_ref, bd_ref, st_ref,
+    )
+
+
 def compose(later, earlier):
     moved = mm(later[:, DV:], earlier)
     return jnp.concatenate([moved[:, :DV] + later[:, :DV], moved[:, DV:]], 1)
@@ -193,10 +212,11 @@
 
 def finish_kernel(
     bits, n_head, steps,
-    out_ref, qeff_ref, trans_ref, gate_ref, gain_ref, weight_ref, mixed_ref,
+    out_ref, qeff_ref, trans_ref, gate_hbm, gain_ref, weight_hbm, mixed_ref,
     start_ref, hid_ref, total_ref, prefix_ref, low_ref, give_ref, got_ref, give_b_ref, got_b_ref,
     give_s_ref, part_ref, up_ref, down_ref,
     state_send, state_recv, part_send, up_recv, down_recv,
+    gate_ref, weight_ref, in_sem,
 ):
     heads = trans_ref.shape[0]
     own = heads // 2
@@ -214,6 +234,10 @@
     def partner(b):
         return {"ctx": me + (1 - 2 * bit(b)) * 2**b}
 
+    gate_copy = pltpu.make_async_copy(gate_hbm, gate_ref, in_sem.at[0])
+    weight_copy = pltpu.make_async_copy(weight_hbm, weight_ref, in_sem.at[1])
+    gate_copy.start()
+    weight_copy.start()
     barrier = pltpu.get_barrier_semaphore()
     for b in range(bits):
         pl.semaphore_signal(
@@ -323,6 +347,8 @@
         )
 
     gain = gain_ref[...]
+    gate_copy.wait()
+    weight_copy.wait()
     for t in range(steps // group):
         at = slice(t * group * rows, (t + 1) * group * rows)
         for h in range(heads):
@@ -432,32 +458,31 @@
         [(i, i + 1) for i in range(n_ctx - 1)],
     )
     vmem = pl.BlockSpec(memory_space=pltpu.VMEM)
+    hbm = pl.BlockSpec(memory_space=pltpu.HBM)
     out, qeff, trans = pl.pallas_call(
-        local_kernel,
+        local_entry,
         out_shape=(
             jax.ShapeDtypeStruct((tokens, heads * DV), F32),
             jax.ShapeDtypeStruct((tokens, heads * DK), BF16),
             jax.ShapeDtypeStruct((heads, DK, DV + DK), BF16),
         ),
-        grid=(1,),
-        in_specs=[
-            pl.BlockSpec(x.shape, lambda i: (0, 0))
-            for x in (
-                query_raw, key_raw, value_raw, rim, conv_query, conv_key, conv_value,
-                decay_log, write_beta,
-            )
-        ],
+        in_specs=[hbm] * 5 + [vmem] * 2,
         out_specs=[vmem] * 3,
         scratch_shapes=[
             pltpu.VMEM((8, channels), F32),
             pltpu.VMEM((ratio * CHUNK, ratio * CHUNK), BF16),
             pltpu.VMEM((heads, DK, DV + DK), F32),
+            *(
+                pltpu.VMEM(x.shape, x.dtype)
+                for x in (query_raw, key_raw, value_raw, decay_log, write_beta)
+            ),
+            pltpu.SemaphoreType.DMA((5,)),
         ],
         compiler_params=pltpu.CompilerParams(vmem_limit_bytes=48 * 2**20),
         name="local",
     )(
-        query_raw, key_raw, value_raw, rim, conv_query, conv_key, conv_value,
-        decay_log, write_beta,
+        query_raw, key_raw, value_raw, decay_log, write_beta, rim,
+        jnp.concatenate([conv_query, conv_key, conv_value], 1).astype(F32),
     )
     bits = n_ctx.bit_length() - 1
     assert n_ctx == 2**bits and bits > 1
@@ -469,7 +494,7 @@
     return pl.pallas_call(
         functools.partial(finish_kernel, bits, n_head, steps),
         out_shape=jax.ShapeDtypeStruct((tokens, features), BF16),
-        in_specs=[vmem] * 6,
+        in_specs=[vmem, vmem, vmem, hbm, vmem, hbm],
         out_specs=vmem,
         scratch_shapes=[
             pltpu.VMEM((heads, DK, DV), BF16),
@@ -490,6 +515,9 @@
             pltpu.SemaphoreType.DMA((n_head, steps)),
             pltpu.SemaphoreType.DMA((n_head, steps)),
             pltpu.SemaphoreType.DMA((n_head, steps)),
+            pltpu.VMEM(gate_input.shape, BF16),
+            pltpu.VMEM(out_weight.shape, BF16),
+            pltpu.SemaphoreType.DMA((2,)),
         ],
         compiler_params=pltpu.CompilerParams(
             vmem_limit_bytes=48 * 2**20, collective_id=0, has_side_effects=True

time: 94.5 us -> 90.5 us (0.958)
  local copies, waits for them, and re-layouts: 11.7 us -> 9.61 us
  Pallas kernels: 78.8 us -> 77 us
    pallas_call x1, Pallas kernels: 64.3 us -> 62.2 us  [body(): pl.pallas_call(functools.partial(finish_kernel, bits, n_head, steps), out...]
    unnamed x21 -> x15, local copies, waits for them, and re-layouts: 9.48 us -> 7.41 us
  transfers between devices with their start and end apart: 1 -> 1, of which waited for: 1 -> 1; matrix products, arithmetic and copies ran while one was open for 0% -> 1% of each run, Pallas kernels for 0% -> 0%
where the time goes in v5:
time: 90.5 us; the launch traced here: 89.9 us
  Pallas kernels  77 us (85%)
  local copies, waits for them, and re-layouts  9.61 us (11%)
  starting transfers between devices  2.36 us (3%)
    pallas_call x1, Pallas kernels, body(): pl.pallas_call(functools.partial(finish_kernel, bits, n_head, steps), out...  62.2 us
    pallas_call x1, Pallas kernels, body(): pl.pallas_call(local_entry, out_shape=(jax.ShapeDtypeStruct((tokens, head...  14.8 us
    unnamed x15, local copies, waits for them, and re-layouts  7.41 us
    ppermute x1, starting transfers between devices, body(): lax.ppermute(jnp.concatenate([x[tokens - RIM:] for x in (query_raw, key_r...  2.36 us
    slice x3, local copies, waits for them, and re-layouts, body(): x[tokens - RIM:]  2.2 us
  transfers between devices with their start and end apart: 1, of which 1 were waited for; matrix products, arithmetic and copies ran while one was open for 1% of the time, Pallas kernels for 0%

profile of v5, /device:TPU:0, one launch (start us, length us, event | category | flops | bytes accessed | tf_op | source)
XLA Modules:
  0.0 89.9 jit_solution(2878622871380968638)
XLA Ops:
  0.0 0.7 slice.9
  0.7 0.7 slice.10
  1.4 0.8 slice.11
  2.2 2.4 %collective-permute-start = (bf16[16,2048]{1,0:T(8,128)(2,1)S(1)}, bf16[16,2048]{1,0:T(8,128)(2,1)S(1)}, u32[]{:S(2)}, u32[]{:S(2)}) collective-permute-start(bf16[16,2048]{1,0:T(8,128)(2,1)S(1)} %pad_maximum_fusion), channel_id=1, source_target_pairs={{0,4},{4,8},{8,12},{12,16},{16,20},{20,24},{24,28},{1,5},{5,9},{9,... | collective-permute-start | bytes 196616 | tf_op jit(solution)/shard_map/ppermute | solution.py:455
  4.6 0.7 maximum_convert_fusion.taps_ref
  5.3 0.1 collective-permute-done.rim_ref
  5.4 0.0 copy-start
  5.5 1.2 %copy-done = bf16[512,1024]{1,0:T(8,128)(2,1)S(1)} copy-done((bf16[512,1024]{1,0:T(8,128)(2,1)S(1)}, bf16[512,1024]{1,0:T(8,128)(2,1)}, u32[]{:S(2)}) %copy-start) | copy-done | bytes 1048600
  6.7 0.0 copy-start.2
  6.7 1.0 %copy-done.2 = bf16[512,512]{1,0:T(8,128)(2,1)S(1)} copy-done((bf16[512,512]{1,0:T(8,128)(2,1)S(1)}, bf16[512,512]{1,0:T(8,128)(2,1)}, u32[]{:S(2)}) %copy-start.2) | copy-done | bytes 524312
  7.7 0.0 copy-start.3
  7.7 1.0 %copy-done.3 = bf16[512,512]{1,0:T(8,128)(2,1)S(1)} copy-done((bf16[512,512]{1,0:T(8,128)(2,1)S(1)}, bf16[512,512]{1,0:T(8,128)(2,1)}, u32[]{:S(2)}) %copy-start.3) | copy-done | bytes 524312
  8.8 0.0 copy-start.4
  8.8 0.7 copy-done.4
  9.5 0.0 copy-start.5
  9.5 0.7 copy-done.5
  10.2 14.8 %local.1 = (f32[512,1024]{1,0:T(8,128)S(1)}, bf16[512,1024]{1,0:T(8,128)(2,1)S(1)}, bf16[8,128,256]{2,1,0:T(8,128)(2,1)S(1)}) custom-call(bf16[512,512]{1,0:T(8,128)(2,1)S(1)} %copy-done.2, bf16[512,512]{1,0:T(8,128)(2,1)S(1)} %copy-done.3, bf16[512,1024]{1,0:T(8,128)(2,1)S(1)} %copy-done, f32[8,512]{1,0:T(8,128)S(1)} %copy-done.4, f32[8,512]{1,0:T(8,128)S(1)} %copy-done.5, ...), custom_call_target="tpu_custom_call" | custom-call | tf_op jit(solution)/shard_map/local/pallas_call | solution.py:462
  25.0 0.0 copy-start.1
  25.0 1.2 %copy-done.1 = bf16[512,1024]{1,0:T(8,128)(2,1)S(1)} copy-done((bf16[512,1024]{1,0:T(8,128)(2,1)S(1)}, bf16[512,1024]{1,0:T(8,128)(2,1)}, u32[]{:S(2)}) %copy-start.1) | copy-done | bytes 1048600
  26.2 0.0 copy-start.6
  26.2 0.7 copy-done.6
  26.9 62.2 %finish.1 = bf16[512,512]{1,0:T(8,128)(2,1)S(1)} custom-call(f32[512,1024]{1,0:T(8,128)S(1)} %get-tuple-element.8.out_ref, bf16[512,1024]{1,0:T(8,128)(2,1)S(1)} %get-tuple-element.9.qeff_ref, bf16[8,128,256]{2,1,0:T(8,128)(2,1)S(1)} %get-tuple-element.10.trans_ref, bf16[512,1024]{1,0:T(8,128)(2,1)S(1)} %copy-done.1, f32[1,128]{1,0:T(1,128)S(1)} %bitcast.1, ...), custom_call_target="tpu_custom_call" | custom-call | tf_op jit(solution)/shard_map/finish/pallas_call | solution.py:494
  89.1 0.8 copy.13
  (1 shorter events, 0.0 us)
Async XLA Ops:
  2.2 3.2 %collective-permute-start = (bf16[16,2048]{1,0:T(8,128)(2,1)S(1)}, bf16[16,2048]{1,0:T(8,128)(2,1)S(1)}, u32[]{:S(2)}, u32[]{:S(2)}) collective-permute-start(bf16[16,2048]{1,0:T(8,128)(2,1)S(1)} %pad_maximum_fusion), channel_id=1, source_target_pairs={{0,4},{4,8},{8,12},{12,16},{16,20},{20,24},{24,28},{1,5},{5,9},{9,... | collective-permute-start | bytes 196616 | tf_op jit(solution)/shard_map/ppermute | solution.py:455
  5.4 1.2 %copy-start = (bf16[512,1024]{1,0:T(8,128)(2,1)S(1)}, bf16[512,1024]{1,0:T(8,128)(2,1)}, u32[]{:S(2)}) copy-start(bf16[512,1024]{1,0:T(8,128)(2,1)} %v_ref.1) | copy-start | bytes 3145732
  6.7 1.0 %copy-start.2 = (bf16[512,512]{1,0:T(8,128)(2,1)S(1)}, bf16[512,512]{1,0:T(8,128)(2,1)}, u32[]{:S(2)}) copy-start(bf16[512,512]{1,0:T(8,128)(2,1)} %q_ref.1) | copy-start | bytes 1572868
  7.7 1.0 %copy-start.3 = (bf16[512,512]{1,0:T(8,128)(2,1)S(1)}, bf16[512,512]{1,0:T(8,128)(2,1)}, u32[]{:S(2)}) copy-start(bf16[512,512]{1,0:T(8,128)(2,1)} %k_ref.1) | copy-start | bytes 1572868
  8.8 0.7 copy-start.4
  9.5 0.7 copy-start.5
  25.0 1.2 %copy-start.1 = (bf16[512,1024]{1,0:T(8,128)(2,1)S(1)}, bf16[512,1024]{1,0:T(8,128)(2,1)}, u32[]{:S(2)}) copy-start(bf16[512,1024]{1,0:T(8,128)(2,1)} %gate_hbm.1) | copy-start | bytes 3145732
  26.2 0.7 copy-start.6

commit v6 on v5

--- a/solution.py
+++ b/solution.py
@@ -222,7 +222,7 @@
     own = heads // 2
     tokens = out_ref.shape[0]
     rows = tokens // steps
-    group = 2
+    group = 4
     width = mixed_ref.shape[1]
     me, z = lax.axis_index("ctx"), lax.axis_index("head")
     core = me % 2
@@ -487,7 +487,7 @@
     bits = n_ctx.bit_length() - 1
     assert n_ctx == 2**bits and bits > 1
     own = heads // 2
-    steps = 8
+    steps = 16
     features = out_weight.shape[1] // n_head
     parts = pltpu.VMEM((n_head, tokens, features), BF16)
     state = pltpu.VMEM((own, DK, DV + DK), F32)

time: 90.5 us -> 105 us (1.16)
  Pallas kernels: 77 us -> 91.5 us
    pallas_call x1, Pallas kernels: 62.2 us -> 76.7 us  [body(): pl.pallas_call(functools.partial(finish_kernel, bits, n_head, steps), out...]
where the time goes in v6:
time: 105 us; the launch traced here: 104 us
  Pallas kernels  91.5 us (87%)
  local copies, waits for them, and re-layouts  9.61 us (9%)
  starting transfers between devices  2.36 us (2%)
    pallas_call x1, Pallas kernels, body(): pl.pallas_call(functools.partial(finish_kernel, bits, n_head, steps), out...  76.7 us
    pallas_call x1, Pallas kernels, body(): pl.pallas_call(local_entry, out_shape=(jax.ShapeDtypeStruct((tokens, head...  14.8 us
    unnamed x15, local copies, waits for them, and re-layouts  7.41 us
    ppermute x1, starting transfers between devices, body(): lax.ppermute(jnp.concatenate([x[tokens - RIM:] for x in (query_raw, key_r...  2.36 us
    slice x3, local copies, waits for them, and re-layouts, body(): x[tokens - RIM:]  2.2 us
  transfers between devices with their start and end apart: 1, of which 1 were waited for; matrix products, arithmetic and copies ran while one was open for 1% of the time, Pallas kernels for 0%

profile of v6, /device:TPU:0, one launch (start us, length us, event | category | flops | bytes accessed | tf_op | source)
XLA Modules:
  0.0 104.4 jit_solution(14114828476052373259)
XLA Ops:
  0.0 0.7 slice.9
  0.7 0.7 slice.10
  1.4 0.8 slice.11
  2.2 2.4 %collective-permute-start = (bf16[16,2048]{1,0:T(8,128)(2,1)S(1)}, bf16[16,2048]{1,0:T(8,128)(2,1)S(1)}, u32[]{:S(2)}, u32[]{:S(2)}) collective-permute-start(bf16[16,2048]{1,0:T(8,128)(2,1)S(1)} %pad_maximum_fusion), channel_id=1, source_target_pairs={{0,4},{4,8},{8,12},{12,16},{16,20},{20,24},{24,28},{1,5},{5,9},{9,... | collective-permute-start | bytes 196616 | tf_op jit(solution)/shard_map/ppermute | solution.py:455
  4.6 0.7 maximum_convert_fusion.taps_ref
  5.3 0.1 collective-permute-done.rim_ref
  5.4 0.0 copy-start
  5.5 1.2 %copy-done = bf16[512,1024]{1,0:T(8,128)(2,1)S(1)} copy-done((bf16[512,1024]{1,0:T(8,128)(2,1)S(1)}, bf16[512,1024]{1,0:T(8,128)(2,1)}, u32[]{:S(2)}) %copy-start) | copy-done | bytes 1048600
  6.7 0.0 copy-start.2
  6.7 1.0 copy-done.2
  7.7 0.0 copy-start.3
  7.7 1.0 copy-done.3
  8.8 0.0 copy-start.4
  8.8 0.7 copy-done.4
  9.5 0.0 copy-start.5
  9.5 0.7 copy-done.5
  10.2 14.8 %local.1 = (f32[512,1024]{1,0:T(8,128)S(1)}, bf16[512,1024]{1,0:T(8,128)(2,1)S(1)}, bf16[8,128,256]{2,1,0:T(8,128)(2,1)S(1)}) custom-call(bf16[512,512]{1,0:T(8,128)(2,1)S(1)} %copy-done.2, bf16[512,512]{1,0:T(8,128)(2,1)S(1)} %copy-done.3, bf16[512,1024]{1,0:T(8,128)(2,1)S(1)} %copy-done, f32[8,512]{1,0:T(8,128)S(1)} %copy-done.4, f32[8,512]{1,0:T(8,128)S(1)} %copy-done.5, ...), custom_call_target="tpu_custom_call" | custom-call | tf_op jit(solution)/shard_map/local/pallas_call | solution.py:462
  25.0 0.0 copy-start.1
  25.0 1.2 %copy-done.1 = bf16[512,1024]{1,0:T(8,128)(2,1)S(1)} copy-done((bf16[512,1024]{1,0:T(8,128)(2,1)S(1)}, bf16[512,1024]{1,0:T(8,128)(2,1)}, u32[]{:S(2)}) %copy-start.1) | copy-done | bytes 1048600
  26.2 0.0 copy-start.6
  26.2 0.7 copy-done.6
  26.9 76.7 %finish.1 = bf16[512,512]{1,0:T(8,128)(2,1)S(1)} custom-call(f32[512,1024]{1,0:T(8,128)S(1)} %get-tuple-element.8.out_ref, bf16[512,1024]{1,0:T(8,128)(2,1)S(1)} %get-tuple-element.9.qeff_ref, bf16[8,128,256]{2,1,0:T(8,128)(2,1)S(1)} %get-tuple-element.10.trans_ref, bf16[512,1024]{1,0:T(8,128)(2,1)S(1)} %copy-done.1, f32[1,128]{1,0:T(1,128)S(1)} %bitcast.1, ...), custom_call_target="tpu_custom_call" | custom-call | tf_op jit(solution)/shard_map/finish/pallas_call | solution.py:494
  103.6 0.8 copy.13
  (1 shorter events, 0.0 us)
Async XLA Ops:
  2.2 3.2 %collective-permute-start = (bf16[16,2048]{1,0:T(8,128)(2,1)S(1)}, bf16[16,2048]{1,0:T(8,128)(2,1)S(1)}, u32[]{:S(2)}, u32[]{:S(2)}) collective-permute-start(bf16[16,2048]{1,0:T(8,128)(2,1)S(1)} %pad_maximum_fusion), channel_id=1, source_target_pairs={{0,4},{4,8},{8,12},{12,16},{16,20},{20,24},{24,28},{1,5},{5,9},{9,... | collective-permute-start | bytes 196616 | tf_op jit(solution)/shard_map/ppermute | solution.py:455
  5.4 1.2 %copy-start = (bf16[512,1024]{1,0:T(8,128)(2,1)S(1)}, bf16[512,1024]{1,0:T(8,128)(2,1)}, u32[]{:S(2)}) copy-start(bf16[512,1024]{1,0:T(8,128)(2,1)} %v_ref.1) | copy-start | bytes 3145732
  6.7 1.0 copy-start.2
  7.7 1.0 copy-start.3
  8.8 0.7 copy-start.4
  9.5 0.7 copy-start.5
  25.0 1.2 %copy-start.1 = (bf16[512,1024]{1,0:T(8,128)(2,1)S(1)}, bf16[512,1024]{1,0:T(8,128)(2,1)}, u32[]{:S(2)}) copy-start(bf16[512,1024]{1,0:T(8,128)(2,1)} %gate_hbm.1) | copy-start | bytes 3145732
  26.2 0.7 copy-start.6
